TPU v7x, 128 devices: a whole 4x4x4 slice. The times are simulated.
128 devices in a mesh: wide: 32 (over y, z, core), narrow: 4 (over x).
Axes of the slice: x: 4, y: 4, z: 4, core: 2. Of those that a mesh axis runs over, the one named last changes fastest.
Arguments:
- teacher: bfloat16 [8192, 8192], P('wide'), may hold values from -6 to 6
- intersection_ids: int32 [32, 4, 8], replicated, may hold values from 0 to 8191, as said below
- slot_counts: int32 [32, 4], replicated, may hold values from 4 to 8, as said below
- intersection_weights: bfloat16 [8, 128, 1024, 1024], P(None, None, 'wide', 'narrow'), may hold values from -0.1875 to 0.1875
- student_input: bfloat16 [64, 1024, 1024], P(None, 'wide', 'narrow'), may hold values from -6 to 6
- terrain_class: int32 [1024, 1024], P('wide', 'narrow'), may hold values from 0 to 15
- conv_first: bfloat16 [128, 64, 3, 3], replicated, may hold values from -0.25 to 0.25
- conv_second: bfloat16 [64, 128, 3, 3], replicated, may hold values from -0.1875 to 0.1875
- class_gain: float32 [16, 128], replicated, may hold values from 0.5 to 2
- class_shift: float32 [16, 128], replicated, may hold values from -3 to 3
Outputs:
- error_field: bfloat16 [64, 1024, 1024], P(None, 'wide', 'narrow')
- grad_first: float32 [128, 64, 3, 3], replicated
- grad_second: float32 [64, 128, 3, 3], replicated
- grad_gain: float32 [16, 128], replicated
- grad_shift: float32 [16, 128], replicated
Inputs may be any that keep to these rules, and one draw needn't show every extreme that they name: `intersection_ids`: block n is held by wide index n // 256. Among the 8 slots of one tile at most 2 name blocks of the same wide index; in every tile (i, j) two of the first 4 slots name blocks held by wide index (i + 16) modulo 32. `slot_counts`: some tile has all 8 slots live.
All inputs are finite; a program needn't handle non-finite values.
Results may differ from a plain program's by a relative error of at most 0.0034.
Values may be sent and summed in bfloat16 or wider, within the bound.
No kernel may reach another device: no remote copies, remote signals or barrier semaphores. Data moves between devices by JAX's collectives and lax.ppermute only.
A program may use at most 192 MiB of HBM per device.

v0:
```python
import jax
import jax.numpy as jnp
from jax import lax
from jax.sharding import PartitionSpec as P


def extended(value, sides, width):
    for axis, dim in sides:
        size, length = (lax.axis_size(axis), value.shape[dim])
        up = [(i, (i + 1) % size) for i in range(size - 1)]
        down = [(j, i) for i, j in up]
        last = lax.slice_in_dim(value, length - width, length, axis=dim)
        initial = lax.slice_in_dim(value, 0, width, axis=dim)
        before = lax.ppermute(last, axis, up)
        after = lax.ppermute(initial, axis, down)
        value = jnp.concatenate([before, value, after], axis=dim)
    return value


def conv_valid(source, kernel):
    return lax.conv_general_dilated(
        source[None],
        kernel,
        (1, 1),
        "VALID",
        dimension_numbers=("NCHW", "OIHW", "NCHW"),
        preferred_element_type=jnp.float32,
    )[0]


def kernel_grad(cotangent, padded):
    outs_ch, height, breadth = cotangent.shape
    in_ch = padded.shape[0]
    flat_cot = cotangent.reshape(outs_ch, height * breadth)
    pieces = []
    for row_off in range(3):
        for col_off in range(3):
            window = padded[:, row_off : row_off + height, col_off : col_off + breadth].reshape(
                in_ch, height * breadth
            )
            pieces.append(
                lax.dot_general(
                    flat_cot, window, (((1,), (1,)), ((), ())), preferred_element_type=jnp.float32
                )
            )
    stacked = jnp.stack(pieces, 0).reshape(3, 3, outs_ch, in_ch)
    return stacked.transpose(2, 3, 0, 1)


def class_sums(onehot_flat, values):
    flat_vals = values.reshape(values.shape[0], -1)
    return lax.dot_general(
        onehot_flat,
        flat_vals,
        (((1,), (1,)), ((), ())),
        precision=lax.Precision.HIGHEST,
        preferred_element_type=jnp.float32,
    )


def shards(
    teacher,
    intersection_ids,
    slot_counts,
    intersection_weights,
    student_input,
    terrain_class,
    conv_first,
    conv_second,
    class_gain,
    class_shift,
):
    band_index = lax.axis_index("wide")
    column_index = lax.axis_index("narrow")
    n_bands = lax.axis_size("wide")
    held = teacher.shape[0]
    slot_total = intersection_ids.shape[2]
    tile_ids = lax.dynamic_index_in_dim(intersection_ids, column_index, 1, keepdims=False)
    tile_counts = lax.dynamic_index_in_dim(slot_counts, column_index, 1, keepdims=False)
    owners = tile_ids // held
    local_rows = tile_ids % held
    positions = lax.broadcasted_iota(jnp.int32, (n_bands, slot_total), 1)
    live = positions < tile_counts[:, None]
    mine = live & (owners == band_index)
    my_owners = lax.dynamic_index_in_dim(owners, band_index, 0, keepdims=False)
    my_live = lax.dynamic_index_in_dim(live, band_index, 0, keepdims=False)
    picked = jnp.take(teacher, local_rows, axis=0)
    outgoing = jnp.where(mine[:, :, None], picked, jnp.zeros((), teacher.dtype))
    incoming = lax.all_to_all(outgoing, "wide", split_axis=0, concat_axis=0, tiled=True)
    blocks = jnp.take_along_axis(incoming, my_owners[None, :, None], axis=0)[0]
    blocks = jnp.where(my_live[:, None], blocks, jnp.zeros((), teacher.dtype))
    cells_block = intersection_weights.shape[1]
    tile_rows = intersection_weights.shape[2]
    tile_cols = intersection_weights.shape[3]
    channels = blocks.shape[1] // cells_block
    flat_blocks = blocks.reshape(slot_total * cells_block, channels)
    flat_weights = intersection_weights.reshape(slot_total * cells_block, tile_rows * tile_cols)
    target = lax.dot_general(
        flat_blocks, flat_weights, (((0,), (0,)), ((), ())), preferred_element_type=jnp.float32
    )
    target = target.reshape(channels, tile_rows, tile_cols)
    input_pad = extended(student_input, (("wide", 1), ("narrow", 2)), 1)
    first = conv_valid(input_pad, conv_first)
    class_total = class_gain.shape[0]
    class_iota = lax.broadcasted_iota(jnp.int32, (class_total, tile_rows, tile_cols), 0)
    onehot = (terrain_class[None] == class_iota).astype(jnp.float32)
    gain_map = jnp.einsum("kj,krc->jrc", class_gain, onehot, precision=lax.Precision.HIGHEST)
    shift_map = jnp.einsum("kj,krc->jrc", class_shift, onehot, precision=lax.Precision.HIGHEST)
    pre = first * gain_map + shift_map
    hidden = (pre * jax.nn.sigmoid(pre)).astype(jnp.bfloat16)
    hidden_pad = extended(hidden, (("wide", 1), ("narrow", 2)), 1)
    second = conv_valid(hidden_pad, conv_second)
    error = student_input.astype(jnp.float32) + second - target
    error_field = error.astype(jnp.bfloat16)
    scaled = (error / (tile_rows * tile_cols)).astype(jnp.bfloat16)
    scaled_pad = extended(scaled, (("wide", 1), ("narrow", 2)), 1)
    flipped = jnp.flip(conv_second, (2, 3)).transpose(1, 0, 2, 3)
    back = conv_valid(scaled_pad, flipped)
    sigma = jax.nn.sigmoid(pre)
    delta = back * (sigma * (1.0 + pre * (1.0 - sigma)))
    onehot_flat = onehot.reshape(class_total, tile_rows * tile_cols)
    shift_term = class_sums(onehot_flat, delta)
    gain_term = class_sums(onehot_flat, delta * first)
    act_cot = (delta * gain_map).astype(jnp.bfloat16)
    first_term = kernel_grad(act_cot, input_pad)
    second_term = kernel_grad(scaled, hidden_pad)
    grad_first, grad_second, grad_gain, grad_shift = lax.psum(
        (first_term, second_term, gain_term, shift_term), ("wide", "narrow")
    )
    return (error_field, grad_first, grad_second, grad_gain, grad_shift)


def solution(mesh):
    in_specs = (
        P("wide", None),
        P(),
        P(),
        P(None, None, "wide", "narrow"),
        P(None, "wide", "narrow"),
        P("wide", "narrow"),
        P(),
        P(),
        P(),
        P(),
    )
    out_specs = (P(None, "wide", "narrow"), P(), P(), P(), P())
    return jax.shard_map(shards, mesh=mesh, in_specs=in_specs, out_specs=out_specs, check_vma=False)
```

profile of v0, /device:TPU:1, one launch (start us, length us, event | category | flops | bytes accessed | tf_op | source)
XLA Modules:
  0.0 453.4 jit_solution(10995793590834354438)
XLA Ops:
  10.4 11.7 %gather_fusion = bf16[256,8192]{1,0:T(8,128)(2,1)} fusion(bf16[256,8192]{1,0:T(8,128)(2,1)} %param.10, s32[1024]{0:T(1024)S(1)} %pad_clamp_fusion), kind=kCustom, calls=%fused_computation | custom fusion | bytes 8389632 | tf_op jit(solution)/shard_map/jit(_take)/gather | solution.py:87
  22.1 4.7 %fusion.4 = bf16[32,8,8192]{2,1,0:T(8,128)(2,1)} fusion(bf16[256,8192]{1,0:T(8,128)(2,1)} %gather_fusion, pred[32,8]{1,0:T(8,128)(4,1)S(1)} %copy.160, pred[32,8]{1,0:T(8,128)(4,1)S(1)} %copy.159), kind=kLoop, calls=%fused_computation.11 | loop fusion | flops 4194304 | bytes 8389120 | tf_op jit(solution)/shard_map/jit(_where)/select_n | solution.py:88
  26.8 9.8 %all-to-all-start = ((bf16[32,8,8192]{2,1,0:T(8,128)(2,1)}), bf16[32,8,8192]{2,1,0:T(8,128)(2,1)}, u32[]{:S(2)}, u32[]{:S(2)}) async-start(bf16[32,8,8192]{2,1,0:T(8,128)(2,1)} %fusion.4), calls=%async_computation | async-start | bytes 8388608 | tf_op jit(solution)/shard_map/all_to_all | solution.py:89
  43.9 5.0 %fusion.124 = f32[32,256,128]{2,1,0:T(8,128)} fusion(s32[32,256]{1,0:T(8,128)S(1)} %copy-done.19, f32[16,128]{1,0:T(8,128)S(1)} %copy-done.28), kind=kOutput, calls=%fused_computation.132 | convolution fusion | flops 201457664 | bytes 4235264 | tf_op jit(solution)/shard_map/kj,krc->jrc/dot_general | solution.py:107
  49.0 34.7 %collective-permute-done = bf16[64,1,256]{2,0,1:T(8,128)(2,1)S(1)} collective-permute-done((bf16[64,1,256]{2,0,1:T(8,128)(2,1)S(1)}, bf16[64,1,256]{2,0,1:T(8,128)(2,1)S(1)}, u32[]{:S(2)}, u32[]{:S(2)}) %collective-permute-start) | collective-permute-done | bytes 32800 | tf_op jit(solution)/shard_map/ppermute | solution.py:14
  95.7 4.8 %reshape.357 = bf16[64,34,1,8,33]{4,3,0,1,2:T(8,128)(2,1)} reshape(bf16[64,34,1,264]{3,0,1,2:T(8,128)(2,1)S(1)} %pad) | data formatting | bytes 2297856 | tf_op jit(solution)/shard_map/conv_general_dilated | solution.py:21
  100.5 6.7 %copy.152 = bf16[64,34,1,8,33]{0,3,4,1,2:T(8,128)(2,1)} copy(bf16[64,34,1,8,33]{4,3,0,1,2:T(8,128)(2,1)} %reshape.357) | data formatting | bytes 2297856 | tf_op jit(solution)/shard_map/conv_general_dilated | solution.py:21
  108.2 4.7 %broadcast_select_fusion.2 = f32[32,8,33,128]{3,1,2,0:T(8,128)S(1)} fusion(pred[8,33]{0,1:T(8,128)(4,1)S(1)} %copy-done.33, bf16[128,64,3,3]{0,1,3,2:T(8,128)(2,1)S(1)} %copy-done.31, bf16[64,34,1,7,2]{0,3,4,1,2:T(8,128)(2,1)S(1)} %slice.142, bf16[64,34,1,8,33]{0,3,4,1,2:T(8,128)(2,1)} %copy.152), kind=kOutput, calls=%fused_computation.43 | convolution fusion | flops 1250445312 | bytes 5682952 | tf_op jit(solution)/shard_map/conv_general_dilated | solution.py:21
  115.1 8.1 %multiply_convert_fusion = (bf16[128,32,256]{0,2,1:T(8,128)(2,1)S(1)}, f32[128,32,256]{0,2,1:T(8,128)}) fusion(f32[16,128]{1,0:T(8,128)S(1)} %copy-done.32, s32[32,256]{1,0:T(8,128)S(1)} %copy-done.19, f32[32,256,128]{2,1,0:T(8,128)S(1)} %copy-done.7, f32[32,1,256,128]{3,0,2,1:T(8,128)S(1)} %slice.143), kind=kOutput, calls=%fused_computation.18 | convolution fusion | flops 208797696 | bytes 14721024 | tf_op jit(solution)/shard_map/kj,krc->jrc/dot_general | solution.py:108
  132.2 5.6 %collective-permute-start.6 = (bf16[128,34,1]{0,2,1:T(2,128)(2,1)}, bf16[128,34,1]{0,2,1:T(2,128)(2,1)}, u32[]{:S(2)}, u32[]{:S(2)}) collective-permute-start(bf16[128,34,1]{0,2,1:T(2,128)(2,1)} %get-tuple-element.36), channel_id=1, source_target_pairs={{0,1},{1,2},{2,3},{4,5},{5,6},{6,7},{8,9},{9,10},{10,11},{12,13},{... | collective-permute-start | bytes 26120 | tf_op jit(solution)/shard_map/ppermute | solution.py:14
  137.9 13.7 %copy.228 = bf16[128,8,32,256]{3,1,2,0:T(8,128)(2,1)} copy(bf16[128,8,32,256]{3,2,1,0:T(8,128)(2,1)S(1)} %bitcast.269) | data formatting | bytes 33554432
  151.6 22.4 %copy.162 = bf16[8192,1024]{1,0:T(8,128)(2,1)} copy(bf16[8192,1024]{0,1:T(8,128)(2,1)} %bitcast.263) | data formatting | bytes 33554432 | tf_op jit(solution)/shard_map/dot_general | solution.py:98
  179.0 4.7 %reshape.289 = bf16[128,34,1,8,33]{0,4,3,1,2:T(8,128)(2,1)} reshape(bf16[128,34,1,264]{0,3,1,2:T(8,128)(2,1)} %pad.2) | data formatting | bytes 4595712 | tf_op jit(solution)/shard_map/conv_general_dilated | solution.py:21
  185.8 5.2 %broadcast_select_fusion = f32[32,8,33,64]{3,1,2,0:T(8,128)S(1)} fusion(pred[8,33]{0,1:T(8,128)(4,1)S(1)} %copy-done.34, bf16[64,128,3,3]{1,0,3,2:T(8,128)(2,1)S(1)} %copy-done, bf16[128,34,1,7,2]{0,3,4,1,2:T(8,128)(2,1)S(1)} %slice.146, bf16[128,34,1,8,33]{0,3,4,1,2:T(8,128)(2,1)S(1)} %copy.156), kind=kOutput, calls=%fused_computation.41 | convolution fusion | flops 1253560320 | bytes 4730120 | tf_op jit(solution)/shard_map/conv_general_dilated | solution.py:21
  194.3 4.6 %copy.226 = f32[32,1,256,64]{2,3,0,1:T(8,128)} copy(f32[32,1,256,64]{3,0,2,1:T(8,128)} %slice.147) | data formatting | bytes 4194304
  198.8 4.6 %pad_maximum_fusion = (bf16[128,34,257]{0,2,1:T(8,128)(2,1)}, bf16[128,34,257]{0,2,1:T(8,128)(2,1)}) fusion(bf16[128,34,1]{0,2,1:T(2,128)(2,1)S(1)} %collective-permute-done.7, bf16[128,1,256]{0,2,1:T(8,128)(2,1)S(1)} %collective-permute-done.5, bf16[128,32,256]{0,2,1:T(8,128)(2,1)S(1)} %get-tuple-element.51, ...), kind=kLoop, calls=%fused_computation.40 | loop fusion | flops 17895424 | bytes 6719488 | tf_op jit(solution)/shard_map/concatenate | solution.py:16
  209.3 13.5 %multiply_convert_fusion.1 = (bf16[64,32,256]{2,0,1:T(8,128)(2,1)}, bf16[64,32,256]{2,0,1:T(8,128)(2,1)}) fusion(bf16[32,256,1024]{2,1,0:T(8,128)(2,1)} %bitcast.262, bf16[1024,64]{1,0:T(8,128)(2,1)} %select_n.132, f32[32,1,256,64]{2,3,0,1:T(8,128)} %copy.226, bf16[64,32,256]{2,1,0:T(8,128)(2,1)} %param.14), kind=kOutput, calls=%fused_computation.64 | convolution fusion | flops 1076887552 | bytes 22151168 | tf_op jit(solution)/shard_map/dot_general | solution.py:98
  255.8 4.8 %reshape.358 = bf16[64,34,1,8,33]{4,3,0,1,2:T(8,128)(2,1)} reshape(bf16[64,34,1,264]{3,0,1,2:T(8,128)(2,1)S(1)} %pad.4) | data formatting | bytes 2297856 | tf_op jit(solution)/shard_map/conv_general_dilated | solution.py:21
  260.6 6.7 %copy.170 = bf16[64,34,1,8,33]{0,3,4,1,2:T(8,128)(2,1)} copy(bf16[64,34,1,8,33]{4,3,0,1,2:T(8,128)(2,1)} %reshape.358) | data formatting | bytes 2297856 | tf_op jit(solution)/shard_map/conv_general_dilated | solution.py:21
  268.2 4.7 %broadcast_select_fusion.1 = f32[32,8,33,128]{3,1,2,0:T(8,128)S(1)} fusion(pred[8,33]{0,1:T(8,128)(4,1)S(1)} %copy-done.35, bf16[64,128,3,3]{1,0,3,2:T(8,128)(2,1)S(1)} %copy-done, bf16[64,34,1,7,2]{0,3,4,1,2:T(8,128)(2,1)S(1)} %slice.154, bf16[64,34,1,8,33]{0,3,4,1,2:T(8,128)(2,1)} %copy.170), kind=kOutput, calls=%fused_computation.42 | convolution fusion | flops 1250445312 | bytes 5682952 | tf_op jit(solution)/shard_map/conv_general_dilated | solution.py:21
  277.3 6.5 %fusion.5 = (bf16[128,32,256]{0,2,1:T(8,128)(2,1)S(1)}, f32[128,32,256]{0,2,1:T(8,128)}) fusion(f32[32,256,128]{2,1,0:T(8,128)S(1)} %copy-done.8, f32[128,32,256]{0,2,1:T(8,128)S(1)} %copy-done.14, f32[32,1,256,128]{3,0,2,1:T(8,128)S(1)} %slice.155), kind=kLoop, calls=%fused_computation.15 | loop fusion | flops 10485760 | bytes 18874368 | tf_op jit(solution)/shard_map/convert_element_type | solution.py:124
  292.2 7.6 %fusion.105 = f32[16,128]{1,0:T(8,128)S(1)} fusion(f32[128,32,256]{0,2,1:T(8,128)} %get-tuple-element.30, f32[32,1,256,128]{3,0,2,1:T(8,128)} %copy-done.6, s32[32,256]{1,0:T(8,128)S(1)} %copy-done.19), kind=kOutput, calls=%fused_computation.115 | convolution fusion | flops 202506240 | bytes 8429568 | tf_op jit(solution)/shard_map/dot_general | solution.py:52
  301.4 70.7 %all-reduce = (f32[16,128]{1,0:T(8,128)}, f32[16,128]{1,0:T(8,128)}) all-reduce(f32[16,128]{1,0:T(8,128)S(1)} %fusion.105, f32[16,128]{1,0:T(8,128)S(1)} %convolution_bitcast_fusion.10), channel_id=1, replica_groups=mesh['wide'=32,'narrow'=4] {'wide','narrow'}, use_global_device_ids=true, to_apply=%region_2.3 | all-reduce | flops 4096 | bytes 32768 | tf_op jit(solution)/shard_map/psum | solution.py:127
  372.1 70.6 %all-reduce.4.cloned.1.call-done = (f32[128,64,3,3]{0,1,3,2:T(8,128)}, f32[64,128,3,3]{1,0,3,2:T(8,128)}) async-done(((f32[128,64,3,3]{0,1,3,2:T(8,128)}, f32[64,128,3,3]{1,0,3,2:T(8,128)}), (f32[128,64,3,3]{0,1,3,2:T(8,128)}, f32[64,128,3,3]{1,0,3,2:T(8,128)})) %all-reduce.4.cloned.1.call-update) | async-done | bytes 589840 | tf_op jit(solution)/shard_map/psum | solution.py:127
  (181 shorter events, 102.1 us)
Async XLA Ops:
  7.2 178.6 %copy-start = (bf16[64,128,3,3]{1,0,3,2:T(8,128)(2,1)S(1)}, bf16[64,128,3,3]{1,0,3,2:T(8,128)(2,1)}, u32[]{:S(2)}) copy-start(bf16[64,128,3,3]{1,0,3,2:T(8,128)(2,1)} %param.17) | copy-start | bytes 442372
  26.8 9.9 %copy-start.4 = (bf16[64,32,256]{2,1,0:T(8,128)(2,1)S(1)}, bf16[64,32,256]{2,1,0:T(8,128)(2,1)}, u32[]{:S(2)}) copy-start(bf16[64,32,256]{2,1,0:T(8,128)(2,1)} %param.14) | copy-start | bytes 3145732
  26.8 17.1 %copy-start.19 = (s32[32,256]{1,0:T(8,128)S(1)}, s32[32,256]{1,0:T(8,128)}, u32[]{:S(2)}) copy-start(s32[32,256]{1,0:T(8,128)} %param.15) | copy-start | bytes 98308
  26.8 17.1 %copy-start.28 = (f32[16,128]{1,0:T(8,128)S(1)}, f32[16,128]{1,0:T(8,128)}, u32[]{:S(2)}) copy-start(f32[16,128]{1,0:T(8,128)} %param.18) | copy-start | bytes 24580
  26.8 176.7 %all-to-all-start = ((bf16[32,8,8192]{2,1,0:T(8,128)(2,1)}), bf16[32,8,8192]{2,1,0:T(8,128)(2,1)}, u32[]{:S(2)}, u32[]{:S(2)}) async-start(bf16[32,8,8192]{2,1,0:T(8,128)(2,1)} %fusion.4), calls=%async_computation | async-start | bytes 8388608 | tf_op jit(solution)/shard_map/all_to_all | solution.py:89
  36.6 406.1 %all-reduce.4.cloned.1.call-start = ((), (), s32[]{:S(2)}) async-start(), calls=%async_computation.1 | async-start | bytes 1179648 | tf_op jit(solution)/shard_map/psum | solution.py:127
  38.2 45.5 %collective-permute-start = (bf16[64,1,256]{2,0,1:T(8,128)(2,1)S(1)}, bf16[64,1,256]{2,0,1:T(8,128)(2,1)S(1)}, u32[]{:S(2)}, u32[]{:S(2)}) collective-permute-start(bf16[64,1,256]{2,0,1:T(8,128)(2,1)S(1)} %get-tuple-element.49), channel_id=1, source_target_pairs={{0,4},{4,8},{8,12},{12,16},{16,20},{20,24},{24,28},{28,32},{32,36}... | collective-permute-start | bytes 98312 | tf_op jit(solution)/shard_map/ppermute | solution.py:14
  41.7 44.3 %collective-permute-start.1 = (bf16[64,1,256]{2,0,1:T(8,128)(2,1)S(1)}, bf16[64,1,256]{2,0,1:T(8,128)(2,1)S(1)}, u32[]{:S(2)}, u32[]{:S(2)}) collective-permute-start(bf16[64,1,256]{2,0,1:T(8,128)(2,1)S(1)} %get-tuple-element.48), channel_id=1, source_target_pairs={{4,0},{8,4},{12,8},{16,12},{20,16},{24,20},{28,24},{32,28},{36,32}... | collective-permute-start | bytes 98312 | tf_op jit(solution)/shard_map/ppermute | solution.py:15
  86.1 9.4 %copy-start.24 = (bf16[64,1,256]{2,0,1:T(8,128)(2,1)}, bf16[64,1,256]{2,0,1:T(8,128)(2,1)S(1)}, u32[]{:S(2)}) copy-start(bf16[64,1,256]{2,0,1:T(8,128)(2,1)S(1)} %collective-permute-done.1) | copy-start | bytes 98308
  86.7 5.6 %collective-permute-start.3 = (bf16[64,34,1]{0,1,2:T(8,128)(2,1)S(1)}, bf16[64,34,1]{0,1,2:T(8,128)(2,1)S(1)}, u32[]{:S(2)}, u32[]{:S(2)}) collective-permute-start(bf16[64,34,1]{0,1,2:T(8,128)(2,1)S(1)} %copy.147), channel_id=1, source_target_pairs={{1,0},{2,1},{3,2},{5,4},{6,5},{7,6},{9,8},{10,9},{11,10},{13,12},{... | collective-permute-start | bytes 13064 | tf_op jit(solution)/shard_map/ppermute | solution.py:15
  88.3 4.8 %collective-permute-start.2 = (bf16[64,34,1]{0,1,2:T(8,128)(2,1)S(1)}, bf16[64,34,1]{0,1,2:T(8,128)(2,1)S(1)}, u32[]{:S(2)}, u32[]{:S(2)}) collective-permute-start(bf16[64,34,1]{0,1,2:T(8,128)(2,1)S(1)} %copy.146), channel_id=1, source_target_pairs={{0,1},{1,2},{2,3},{4,5},{5,6},{6,7},{8,9},{9,10},{10,11},{12,13},{... | collective-permute-start | bytes 13064 | tf_op jit(solution)/shard_map/ppermute | solution.py:14
  113.8 24.1 %slice-start = ((s8[16777216]{0:T(1024)(128)(4,1)}), s8[4194304]{0:T(1024)(128)(4,1)S(1)}, s32[]{:S(2)}) async-start(s8[16777216]{0:T(1024)(128)(4,1)} %bitcast.267), calls=%async_computation.2 | async-start | bytes 8388608
  113.8 24.1 %slice-start.1 = ((s8[16777216]{0:T(1024)(128)(4,1)}), s8[4194304]{0:T(1024)(128)(4,1)S(1)}, s32[]{:S(2)}) async-start(s8[16777216]{0:T(1024)(128)(4,1)} %bitcast.267), calls=%async_computation.3 | async-start | bytes 8388608
  115.1 22.8 %slice-start.2 = ((s8[16777216]{0:T(1024)(128)(4,1)}), s8[4194304]{0:T(1024)(128)(4,1)S(1)}, s32[]{:S(2)}) async-start(s8[16777216]{0:T(1024)(128)(4,1)} %bitcast.267), calls=%async_computation.4 | async-start | bytes 8388608
  115.1 22.8 %slice-start.3 = ((s8[16777216]{0:T(1024)(128)(4,1)}), s8[4194304]{0:T(1024)(128)(4,1)S(1)}, s32[]{:S(2)}) async-start(s8[16777216]{0:T(1024)(128)(4,1)} %bitcast.267), calls=%async_computation.5 | async-start | bytes 8388608
  123.2 5.9 %collective-permute-start.5 = (bf16[128,1,256]{0,2,1:T(8,128)(2,1)S(1)}, bf16[128,1,256]{0,2,1:T(8,128)(2,1)S(1)}, u32[]{:S(2)}, u32[]{:S(2)}) collective-permute-start(bf16[128,1,256]{0,2,1:T(8,128)(2,1)S(1)} %get-tuple-element.41), channel_id=1, source_target_pairs={{4,0},{8,4},{12,8},{16,12},{20,16},{24,20},{28,24},{32,28},{36,32}... | collective-permute-start | bytes 196616 | tf_op jit(solution)/shard_map/ppermute | solution.py:15
  125.1 5.2 %collective-permute-start.4 = (bf16[128,1,256]{0,2,1:T(8,128)(2,1)S(1)}, bf16[128,1,256]{0,2,1:T(8,128)(2,1)S(1)}, u32[]{:S(2)}, u32[]{:S(2)}) collective-permute-start(bf16[128,1,256]{0,2,1:T(8,128)(2,1)S(1)} %get-tuple-element.40), channel_id=1, source_target_pairs={{0,4},{4,8},{8,12},{12,16},{16,20},{20,24},{24,28},{28,32},{32,36}... | collective-permute-start | bytes 196616 | tf_op jit(solution)/shard_map/ppermute | solution.py:14
  131.0 43.8 %collective-permute-start.7 = (bf16[128,34,1]{0,2,1:T(2,128)(2,1)}, bf16[128,34,1]{0,2,1:T(2,128)(2,1)S(1)}, u32[]{:S(2)}, u32[]{:S(2)}) collective-permute-start(bf16[128,34,1]{0,2,1:T(2,128)(2,1)} %get-tuple-element.37), channel_id=1, source_target_pairs={{1,0},{2,1},{3,2},{5,4},{6,5},{7,6},{9,8},{10,9},{11,10},{13,12},{... | collective-permute-start | bytes 26120 | tf_op jit(solution)/shard_map/ppermute | solution.py:15
  132.2 42.5 %collective-permute-start.6 = (bf16[128,34,1]{0,2,1:T(2,128)(2,1)}, bf16[128,34,1]{0,2,1:T(2,128)(2,1)}, u32[]{:S(2)}, u32[]{:S(2)}) collective-permute-start(bf16[128,34,1]{0,2,1:T(2,128)(2,1)} %get-tuple-element.36), channel_id=1, source_target_pairs={{0,1},{1,2},{2,3},{4,5},{5,6},{6,7},{8,9},{9,10},{10,11},{12,13},{... | collective-permute-start | bytes 26120 | tf_op jit(solution)/shard_map/ppermute | solution.py:14
  222.8 9.8 %copy-start.2 = (bf16[64,32,256]{2,0,1:T(8,128)(2,1)S(1)}, bf16[64,32,256]{2,0,1:T(8,128)(2,1)}, u32[]{:S(2)}) copy-start(bf16[64,32,256]{2,0,1:T(8,128)(2,1)} %get-tuple-element.38) | copy-start | bytes 3145732
  223.6 14.5 %collective-permute-start.9 = (bf16[64,1,256]{2,0,1:T(8,128)(2,1)S(1)}, bf16[64,1,256]{2,0,1:T(8,128)(2,1)S(1)}, u32[]{:S(2)}, u32[]{:S(2)}) collective-permute-start(bf16[64,1,256]{2,0,1:T(8,128)(2,1)S(1)} %get-tuple-element.47), channel_id=1, source_target_pairs={{4,0},{8,4},{12,8},{16,12},{20,16},{24,20},{28,24},{32,28},{36,32}... | collective-permute-start | bytes 98312 | tf_op jit(solution)/shard_map/ppermute | solution.py:15
  225.6 13.2 %collective-permute-start.8 = (bf16[64,1,256]{2,0,1:T(8,128)(2,1)S(1)}, bf16[64,1,256]{2,0,1:T(8,128)(2,1)S(1)}, u32[]{:S(2)}, u32[]{:S(2)}) collective-permute-start(bf16[64,1,256]{2,0,1:T(8,128)(2,1)S(1)} %get-tuple-element.46), channel_id=1, source_target_pairs={{0,4},{4,8},{8,12},{12,16},{16,20},{20,24},{24,28},{28,32},{32,36}... | collective-permute-start | bytes 98312 | tf_op jit(solution)/shard_map/ppermute | solution.py:14
  240.4 11.5 %collective-permute-start.11 = (bf16[64,34,1]{0,1,2:T(8,128)(2,1)S(1)}, bf16[64,34,1]{0,1,2:T(8,128)(2,1)S(1)}, u32[]{:S(2)}, u32[]{:S(2)}) collective-permute-start(bf16[64,34,1]{0,1,2:T(8,128)(2,1)S(1)} %copy.165), channel_id=1, source_target_pairs={{1,0},{2,1},{3,2},{5,4},{6,5},{7,6},{9,8},{10,9},{11,10},{13,12},{... | collective-permute-start | bytes 13064 | tf_op jit(solution)/shard_map/ppermute | solution.py:15
  243.1 9.2 %collective-permute-start.10 = (bf16[64,34,1]{0,1,2:T(8,128)(2,1)S(1)}, bf16[64,34,1]{0,1,2:T(8,128)(2,1)S(1)}, u32[]{:S(2)}, u32[]{:S(2)}) collective-permute-start(bf16[64,34,1]{0,1,2:T(8,128)(2,1)S(1)} %copy.164), channel_id=1, source_target_pairs={{0,1},{1,2},{2,3},{4,5},{5,6},{6,7},{8,9},{9,10},{10,11},{12,13},{... | collective-permute-start | bytes 13064 | tf_op jit(solution)/shard_map/ppermute | solution.py:14
  (30 other events, 109.6 us)
Sparse Core Ops, SparseCore 0:
  292.3 150.3 all-reduce.3
where the time goes:
time: 463 us; the launch traced here: 453 us
  local copies, waits for them, and re-layouts  121 us (26%)
  waiting for transfers between devices  109 us (24%)
  blocking collectives  70.7 us (15%)
  matrix products  65.6 us (14%)
  starting transfers between devices  45.4 us (10%)
  other arithmetic  27 us (6%)
  between operations  15.3 us (3%)
    psum x1, blocking collectives, shards(): lax.psum((first_term, second_term, gain_term, shift_term), ('wide', 'narr...  70.7 us
    psum x1, waiting for transfers between devices, shards(): lax.psum((first_term, second_term, gain_term, shift_term), ('wide', 'narr...  70.6 us
    conv_general_dilated x15, local copies, waits for them, and re-layouts, conv_valid(): lax.conv_general_dilated(source[None], kernel, (1, 1), 'VALID', dimension...  37.5 us
    ppermute x6, waiting for transfers between devices, extended(): before = lax.ppermute(last, axis, up)  36.4 us
    unnamed x89, local copies, waits for them, and re-layouts  34.7 us
    ppermute x6, starting transfers between devices, extended(): before = lax.ppermute(last, axis, up)  25.7 us
    dot_general x1, local copies, waits for them, and re-layouts, shards(): lax.dot_general(flat_blocks, flat_weights, (((0,), (0,)), ((), ())), pref...  22.4 us
    dot_general x18, matrix products, kernel_grad(): lax.dot_general(flat_cot, window, (((1,), (1,)), ((), ())), preferred_ele...  15.3 us
  transfers between devices with their start and end apart: 14, of which 5 were waited for; matrix products, arithmetic and copies ran while one was open for 27% of the time, Pallas kernels for 0%

commit v1 on v0

v1 whole, which is shorter than its diff:
```python
import jax
import jax.numpy as jnp
from jax import lax
from jax.experimental import pallas as pl
from jax.experimental.pallas import tpu as pltpu
from jax.sharding import PartitionSpec as P

F32 = jnp.float32
BF16 = jnp.bfloat16
VMEM_LIMIT = 56 * 1024 * 1024
CX = 80
WIDE_ROW = 384


def whole():
    return pl.BlockSpec(memory_space=pltpu.VMEM)


def nt(a, b):
    return lax.dot_general(a, b, (((1,), (1,)), ((), ())), preferred_element_type=F32)


def dot(a, b):
    return jnp.dot(a, b, preferred_element_type=F32)


def iota(shape, dim):
    return lax.broadcasted_iota(jnp.int32, shape, dim)


def params():
    return pltpu.CompilerParams(vmem_limit_bytes=VMEM_LIMIT)


def pack_columns(mid, top, bottom, width):
    rows, channels, cols = mid.shape
    span = 128 // width

    def body(mid_ref, top_ref, bottom_ref, out_ref, acc_ref):
        q = iota((cols, 256), 0)
        lane = iota((cols, 256), 1)
        part = (lane % 128) // span
        source = jnp.where(lane < 128, part, cols - width + part)
        base = jnp.where(q == source, 1.0, 0.0).astype(BF16)
        place = iota((channels, 256), 1) % span
        acc_ref[...] = jnp.zeros_like(acc_ref)

        def put(row, value):
            picked = dot(value, base)
            acc_ref[...] = jnp.where(place == row, picked, acc_ref[...])

        for k in range(width):
            put(k, top_ref[k])
            put(width + rows + k, bottom_ref[k])

        def step(r, carry):
            put(r + width, mid_ref[r])
            return carry

        lax.fori_loop(0, rows, step, 0)
        out_ref[0] = acc_ref[:, :128].astype(BF16)
        out_ref[1] = acc_ref[:, 128:].astype(BF16)

    return pl.pallas_call(
        body,
        out_shape=jax.ShapeDtypeStruct((2, channels, 128), BF16),
        in_specs=[whole()] * 3,
        out_specs=whole(),
        scratch_shapes=[pltpu.VMEM((channels, 256), F32)],
        compiler_params=params(),
        name="pack_columns",
    )(mid, top, bottom)


def forward_body(
    mid_ref, top_ref, bottom_ref, left_ref, right_ref, w1_ref, gs_ref, w2_ref,
    xs_ref, first_ref, slope_ref, hidden_ref, onehot_ref, total_ref, hs_ref,
):
    rows = mid_ref.shape[0]
    k_io = iota((256, 128), 0)
    l_io = iota((256, 128), 1)
    k_part = (k_io % 128) // 64
    halo_lane = jnp.where(k_io < 128, 126 + k_part, k_part)
    base = jnp.where(l_io == halo_lane, 1.0, 0.0).astype(BF16)
    place = iota((CX, 256), 1) % 64
    sides = jnp.concatenate([left_ref[...], right_ref[...]], axis=1).astype(F32)

    def build(row, own):
        chosen = jnp.where(place == row, sides, 0.0).astype(BF16)
        halo = dot(chosen, base)
        full = jnp.concatenate([own.astype(F32), halo], axis=1)
        terrain = full[64:72]
        data = full[:64]
        at = pl.multiple_of(row * 208, 16)
        xs_ref[pl.ds(at, 64), :] = pltpu.roll(data, 1, 1).astype(BF16)
        xs_ref[pl.ds(at + 64, 64), :] = data.astype(BF16)
        xs_ref[pl.ds(at + 128, 64), :] = pltpu.roll(data, WIDE_ROW - 1, 1).astype(BF16)
        cls = jnp.broadcast_to(terrain[0:1], (16, WIDE_ROW))
        hot = cls == (iota((16, WIDE_ROW), 0) + 1).astype(F32)
        xs_ref[pl.ds(at + 192, 16), :] = jnp.where(hot, 1.0, 0.0).astype(BF16)

    for k in range(2):
        build(k, top_ref[k])
        build(rows + 2 + k, bottom_ref[k])

    def build_mid(r, carry):
        build(r + 2, mid_ref[r])
        return carry

    lax.fori_loop(0, rows, build_mid, 0)

    gs = gs_ref[...]
    high = gs.astype(BF16).astype(F32)
    middle = (gs - high).astype(BF16).astype(F32)
    low = gs - high - middle
    lane = iota(gs.shape, 1)
    split = jnp.where(lane < 16, high, jnp.where(lane < 32, middle, low)).astype(BF16)

    def activate(h):
        pieces = [xs_ref[pl.ds(pl.multiple_of((h + a) * 208, 16), 192), :] for a in range(3)]
        first = dot(w1_ref[...], jnp.concatenate(pieces, axis=0))
        hot = xs_ref[pl.ds(pl.multiple_of((h + 1) * 208 + 192, 16), 16), :]
        table = dot(split, jnp.concatenate([hot, hot, hot], axis=0))
        gain, shift = table[:128], table[128:]
        pre = first * gain + shift
        sigma = 1.0 / (1.0 + jnp.exp(-pre))
        hidden = pre * sigma
        at = pl.multiple_of(h * 384, 16)
        hs_ref[pl.ds(at, 128), :] = pltpu.roll(hidden, 1, 1)[:, :256].astype(BF16)
        center = hidden[:, :256].astype(BF16)
        hs_ref[pl.ds(at + 128, 128), :] = center
        hs_ref[pl.ds(at + 256, 128), :] = pltpu.roll(hidden, WIDE_ROW - 1, 1)[:, :256].astype(BF16)
        return first, pre, sigma, center, hot

    activate(0)
    activate(rows + 1)

    def own_row(r, carry):
        first, pre, sigma, center, hot = activate(r + 1)
        first_ref[r] = first[:, :256]
        pre, sigma = pre[:, :256], sigma[:, :256]
        slope_ref[r] = sigma * (1.0 + pre * (1.0 - sigma))
        hidden_ref[r] = center
        onehot_ref[r] = hot[:, :256]
        return carry

    lax.fori_loop(0, rows, own_row, 0)

    def second_row(r, carry):
        stack = hs_ref[pl.ds(pl.multiple_of(r * 384, 16), 1152), :]
        total_ref[r] = dot(w2_ref[...], stack) + mid_ref[r][:64].astype(F32)
        return carry

    lax.fori_loop(0, rows, second_row, 0)


def forward(mid, top, bottom, left, right, w1, gs, w2):
    rows = mid.shape[0]
    return pl.pallas_call(
        forward_body,
        out_shape=(
            jax.ShapeDtypeStruct(((rows + 4) * 208, WIDE_ROW), BF16),
            jax.ShapeDtypeStruct((rows, 128, 256), F32),
            jax.ShapeDtypeStruct((rows, 128, 256), F32),
            jax.ShapeDtypeStruct((rows, 128, 256), BF16),
            jax.ShapeDtypeStruct((rows, 16, 256), BF16),
            jax.ShapeDtypeStruct((rows, 64, 256), F32),
        ),
        in_specs=[whole()] * 8,
        out_specs=(whole(),) * 6,
        scratch_shapes=[pltpu.VMEM(((rows + 2) * 384, 256), BF16)],
        compiler_params=params(),
        name="forward",
    )(mid, top, bottom, left, right, w1, gs, w2)


def error_body(blocks_ref, weights_ref, total_ref, error_ref):
    for r in range(weights_ref.shape[0]):
        target = dot(blocks_ref[...], weights_ref[r])
        error_ref[r] = (total_ref[r] - target).astype(BF16)


def error_rows(blocks, weights, total):
    rows, channels, cols = total.shape
    depth = weights.shape[1]
    step = 4
    return pl.pallas_call(
        error_body,
        grid=(rows // step,),
        in_specs=[
            pl.BlockSpec((channels, depth), lambda i: (0, 0)),
            pl.BlockSpec((step, depth, cols), lambda i: (i, 0, 0)),
            pl.BlockSpec((step, channels, cols), lambda i: (i, 0, 0)),
        ],
        out_specs=pl.BlockSpec((step, channels, cols), lambda i: (i, 0, 0)),
        out_shape=jax.ShapeDtypeStruct((rows, channels, cols), BF16),
        compiler_params=params(),
        name="error_rows",
    )(blocks, weights, total)


def backward_body(
    scale, err_ref, top_ref, bottom_ref, left_ref, right_ref, xs_ref, first_ref, slope_ref,
    hidden_ref, onehot_ref, wb_ref, gain_ref, g1_ref, g2_ref, cls_ref, es_ref,
):
    rows = err_ref.shape[0]
    step_rows = first_ref.shape[0]
    step = pl.program_id(0)

    @pl.when(step == 0)
    def _():
        k_io = iota((256, 256), 0)
        l_io = iota((256, 256), 1)
        base = jnp.where(l_io == jnp.where(k_io < 128, 0, 255), 1.0, 0.0).astype(BF16)
        place = iota((64, 256), 1) % 128
        lane = iota((64, 256), 1)
        sides = jnp.concatenate([left_ref[...], right_ref[...]], axis=1).astype(F32)

        def build(row, own):
            halo = dot(jnp.where(place == row, sides, 0.0).astype(BF16), base)
            data = own.astype(F32)
            at = pl.multiple_of(row * 192, 16)
            es_ref[pl.ds(at, 64), :] = jnp.where(lane == 0, halo, pltpu.roll(data, 1, 1)).astype(BF16)
            es_ref[pl.ds(at + 64, 64), :] = own
            es_ref[pl.ds(at + 128, 64), :] = jnp.where(lane == 255, halo, pltpu.roll(data, 255, 1)).astype(BF16)

        build(0, top_ref[0])
        build(rows + 1, bottom_ref[0])

        def build_mid(r, carry):
            build(r + 1, err_ref[r])
            return carry

        lax.fori_loop(0, rows, build_mid, 0)
        g1_ref[...] = jnp.zeros_like(g1_ref)
        g2_ref[...] = jnp.zeros_like(g2_ref)
        cls_ref[...] = jnp.zeros_like(cls_ref)

    gains = gain_ref[...]
    high = gains.astype(BF16).astype(F32)
    middle = (gains - high).astype(BF16).astype(F32)
    low = gains - high - middle
    lane48 = iota(gains.shape, 1)
    split = jnp.where(lane48 < 16, high, jnp.where(lane48 < 32, middle, low)).astype(BF16)

    acc1, acc2, acc3 = g1_ref[...], g2_ref[...], cls_ref[...]
    for k in range(step_rows):
        r = step * step_rows + k
        stack = es_ref[pl.ds(pl.multiple_of(r * 192, 16), 576), :]
        back = dot(wb_ref[...], stack)
        delta = back * slope_ref[k] * scale
        hot = onehot_ref[k]
        gain = dot(split, jnp.concatenate([hot, hot, hot], axis=0))
        act = (delta * gain).astype(BF16)
        scaled_first = delta * first_ref[k]
        d_high = delta.astype(BF16)
        d_low = (delta - d_high.astype(F32)).astype(BF16)
        f_high = scaled_first.astype(BF16)
        f_low = (scaled_first - f_high.astype(F32)).astype(BF16)
        acc3 += nt(hot, jnp.concatenate([d_high, d_low, f_high, f_low], axis=0))
        pieces = [xs_ref[pl.ds(pl.multiple_of((r + 1 + a) * 208, 16), 192), pl.ds(0, 256)] for a in range(3)]
        acc1 += nt(act, jnp.concatenate(pieces, axis=0))
        acc2 += nt(hidden_ref[k], stack)
    g1_ref[...] = acc1
    g2_ref[...] = acc2
    cls_ref[...] = acc3


def backward(scale, err, top, bottom, left, right, xs, first, slope, hidden, onehot, wb, gains):
    rows = err.shape[0]
    step = 4

    def const(shape):
        return pl.BlockSpec(shape, lambda i: (0,) * len(shape))

    def moving(shape):
        return pl.BlockSpec((step,) + shape[1:], lambda i: (i, 0, 0))

    def body(*refs):
        backward_body(scale, *refs)

    return pl.pallas_call(
        body,
        grid=(rows // step,),
        in_specs=[
            const(err.shape), const(top.shape), const(bottom.shape), const(left.shape), const(right.shape),
            const(xs.shape), moving(first.shape), moving(slope.shape), moving(hidden.shape),
            moving(onehot.shape), const(wb.shape), const(gains.shape),
        ],
        out_specs=(const((128, 576)), const((128, 576)), const((16, 512))),
        out_shape=(
            jax.ShapeDtypeStruct((128, 576), F32),
            jax.ShapeDtypeStruct((128, 576), F32),
            jax.ShapeDtypeStruct((16, 512), F32),
        ),
        scratch_shapes=[pltpu.VMEM(((rows + 2) * 192, 256), BF16)],
        compiler_params=params(),
        name="backward",
    )(err, top, bottom, left, right, xs, first, slope, hidden, onehot, wb, gains)


def shifts(axis):
    size = lax.axis_size(axis)
    up = [(i, i + 1) for i in range(size - 1)]
    down = [(i + 1, i) for i in range(size - 1)]
    return up, down


def row_halo(mid, width):
    up, down = shifts("wide")
    top = lax.ppermute(mid[mid.shape[0] - width :], "wide", up)
    bottom = lax.ppermute(mid[:width], "wide", down)
    return top, bottom


def column_halo(packed):
    up, down = shifts("narrow")
    left = lax.ppermute(packed[1], "narrow", up)
    right = lax.ppermute(packed[0], "narrow", down)
    return left, right


def split3(value):
    high = lax.reduce_precision(value, 8, 7)
    middle = lax.reduce_precision(value - high, 8, 7)
    low = value - high - middle
    return high.astype(BF16), middle.astype(BF16), low.astype(BF16)


def everywhere_sum(grads, classes):
    axes = ("wide", "narrow")
    n = lax.axis_size(axes)

    def lay_out(main, small):
        parts = [p.reshape(n, -1) for p in split3(small)]
        row = jnp.concatenate([main.astype(BF16).reshape(n, -1)] + parts, axis=1)
        room = -row.shape[1] % 128
        return jnp.pad(row, ((0, 0), (0, room))).reshape(n, -1, 128)

    def read_back(table, n_main, n_small):
        flat = table.reshape(table.shape[0], -1)
        main = flat[:, :n_main]
        parts = flat[:, n_main : n_main + 3 * n_small].reshape(table.shape[0], 3, n_small)
        return main, parts.sum(1)

    n_main, n_small = grads.size // n, classes.size // n
    got = lax.all_to_all(lay_out(grads, classes), axes, 0, 0, tiled=True)
    total = got.astype(F32).sum(0)
    main, small = read_back(total[None], n_main, n_small)
    parts = split3(small)
    row = jnp.concatenate([main.astype(BF16)] + list(parts), axis=1)
    row = jnp.pad(row, ((0, 0), (0, -row.shape[1] % 128))).reshape(1, -1, 128)
    spread = lax.all_to_all(jnp.broadcast_to(row, (n,) + row.shape[1:]), axes, 0, 0, tiled=True)
    main, small = read_back(spread.astype(F32), n_main, n_small)
    return main.reshape(grads.shape), small.reshape(classes.shape)


def shards(
    teacher,
    intersection_ids,
    slot_counts,
    intersection_weights,
    student_input,
    terrain_class,
    conv_first,
    conv_second,
    class_gain,
    class_shift,
):
    band = lax.axis_index("wide")
    column = lax.axis_index("narrow")
    n_bands = lax.axis_size("wide")
    held = teacher.shape[0]
    slots = intersection_ids.shape[2]
    depth = intersection_weights.shape[1]
    rows, cols = student_input.shape[1:]

    terrain = (terrain_class + 1).astype(BF16)[:, None, :]
    mid = jnp.concatenate(
        [student_input.transpose(1, 0, 2), jnp.pad(terrain, ((0, 0), (0, CX - 65), (0, 0)))], axis=1
    )
    top, bottom = row_halo(mid, 2)
    left, right = column_halo(pack_columns(mid, top, bottom, 2))

    ids = lax.dynamic_index_in_dim(intersection_ids, column, 1, keepdims=False)
    counts = lax.dynamic_index_in_dim(slot_counts, column, 1, keepdims=False)
    owner, local = ids // held, ids % held
    slot = lax.broadcasted_iota(jnp.int32, (n_bands, slots), 1)
    live = slot < counts[:, None]
    same = (owner[:, :, None] == owner[:, None, :]) & live[:, None, :]
    rank = (same & (slot[:1, None, :] < slot[:1, :, None])).sum(-1)
    which = lax.broadcasted_iota(jnp.int32, (n_bands, 2, slots), 1)
    mine = (live & (owner == band))[:, None, :] & (rank[:, None, :] == which)
    pick = (mine[..., None] & (local[:, None, :, None] == jnp.arange(held))).any(2)
    outgoing = dot(pick.reshape(2 * n_bands, held).astype(BF16), teacher).astype(BF16)
    outgoing, left, right = lax.optimization_barrier((outgoing, left, right))
    incoming = lax.all_to_all(
        outgoing.reshape(n_bands, 2, -1), "wide", split_axis=0, concat_axis=0, tiled=True
    )

    weights = intersection_weights.reshape(slots * depth, rows, cols).transpose(1, 0, 2)

    w1 = conv_first.transpose(0, 2, 3, 1).reshape(128, 576)
    w2 = conv_second.transpose(0, 2, 3, 1).reshape(64, 1152)
    wb = jnp.flip(conv_second, (2, 3)).transpose(1, 2, 3, 0).reshape(128, 576)
    gain3 = jnp.tile(class_gain.T, (1, 3))
    gs = jnp.concatenate([gain3, jnp.tile(class_shift.T, (1, 3))], axis=0)
    xs, first, slope, hidden, onehot, total = forward(mid, top, bottom, left, right, w1, gs, w2)

    my_owner = lax.dynamic_index_in_dim(owner, band, 0, keepdims=False)
    my_live = lax.dynamic_index_in_dim(live, band, 0, keepdims=False)
    my_rank = lax.dynamic_index_in_dim(rank, band, 0, keepdims=False)
    pair = lax.broadcasted_iota(jnp.int32, (slots, 2 * n_bands), 1)
    take = ((pair == (my_owner * 2 + my_rank)[:, None]) & my_live[:, None]).astype(BF16)
    blocks = dot(take, incoming.reshape(2 * n_bands, -1)).astype(BF16)
    blocks = blocks.reshape(slots * depth, -1).T

    err = error_rows(blocks, weights, total)
    error_field = err.transpose(1, 0, 2)
    e_top, e_bottom = row_halo(err, 1)
    e_left, e_right = column_halo(pack_columns(err, e_top, e_bottom, 1))
    scale = 1.0 / (rows * cols)
    g1, g2, cls = backward(
        scale, err, e_top, e_bottom, e_left, e_right, xs, first, slope, hidden, onehot, wb, gain3
    )
    classes = jnp.concatenate([cls[:, :128] + cls[:, 128:256], cls[:, 256:384] + cls[:, 384:]], axis=1)
    grads, classes = everywhere_sum(jnp.concatenate([g1, g2 * scale], axis=1), classes)
    grad_first = grads[:, :576].reshape(128, 3, 3, 64).transpose(0, 3, 1, 2)
    grad_second = jnp.flip(grads[:, 576:].reshape(128, 3, 3, 64), (1, 2)).transpose(3, 0, 1, 2)
    return (error_field, grad_first, grad_second, classes[:, 128:], classes[:, :128])


def solution(mesh):
    in_specs = (
        P("wide", None),
        P(),
        P(),
        P(None, None, "wide", "narrow"),
        P(None, "wide", "narrow"),
        P("wide", "narrow"),
        P(),
        P(),
        P(),
        P(),
    )
    out_specs = (P(None, "wide", "narrow"), P(), P(), P(), P())
    return jax.shard_map(shards, mesh=mesh, in_specs=in_specs, out_specs=out_specs, check_vma=False)
```

time: 463 us -> 212 us (0.46); the launches traced: 453 us -> 211 us
  waiting for transfers between devices: 109 us -> 20.3 us
  Pallas kernels: 0 us -> 88.2 us
  local copies, waits for them, and re-layouts: 121 us -> 35.5 us
  matrix products: 65.6 us -> 3.33 us
  blocking collectives: 70.7 us -> 24 us
  other arithmetic: 27 us -> 4.79 us
  between operations: 15.3 us -> 1.13 us
  starting transfers between devices: 45.4 us -> 33.9 us
    pallas_call x0 -> x5, Pallas kernels: none -> 88.2 us  [the longest x1 37.8 us: forward(): pl.pallas_call(forward_body, out_shape=(jax.ShapeDtypeStruct(((rows + 4)...]
    psum x1 -> x0, blocking collectives: 70.7 us -> none  [shards(): lax.psum((first_term, second_term, gain_term, shift_term), ('wide', 'narr...]
    psum x1 -> x0, waiting for transfers between devices: 70.6 us -> none  [shards(): lax.psum((first_term, second_term, gain_term, shift_term), ('wide', 'narr...]
    dot_general x23 -> x2, matrix products: 51 us -> 3.33 us  [dot(): return jnp.dot(a, b, preferred_element_type=F32)]
    conv_general_dilated x15 -> x0, local copies, waits for them, and re-layouts: 37.5 us -> none  [conv_valid(): lax.conv_general_dilated(source[None], kernel, (1, 1), 'VALID', dimension...]
    ppermute x12 -> x8, waiting for transfers between devices: 38.1 us -> 7.65 us  [the longest x2 5.91 us: row_halo(): bottom = lax.ppermute(mid[:width], 'wide', down)]
    all_to_all x0 -> x1, blocking collectives: none -> 24 us  [everywhere_sum(): got = lax.all_to_all(lay_out(grads, classes), axes, 0, 0, tiled=True)]
    dot_general x1 -> x0, local copies, waits for them, and re-layouts: 22.4 us -> none  [shards(): lax.dot_general(flat_blocks, flat_weights, (((0,), (0,)), ((), ())), pref...]
  transfers between devices with their start and end apart: 14 -> 10, of which waited for: 5 -> 5; matrix products, arithmetic and copies ran while one was open for 27% -> 12% of each run, Pallas kernels for 0% -> 18%
where the time goes in v1:
time: 212 us; the launch traced here: 211 us
  Pallas kernels  88.2 us (42%)
  local copies, waits for them, and re-layouts  35.5 us (17%)
  starting transfers between devices  33.9 us (16%)
  blocking collectives  24 us (11%)
  waiting for transfers between devices  20.3 us (10%)
  other arithmetic  4.79 us (2%)
  matrix products  3.33 us (2%)
    pallas_call x1, Pallas kernels, forward(): pl.pallas_call(forward_body, out_shape=(jax.ShapeDtypeStruct(((rows + 4)...  37.8 us
    pallas_call x1, Pallas kernels, backward(): pl.pallas_call(body, grid=(rows // step,), in_specs=[const(err.shape), co...  25.7 us
    all_to_all x1, blocking collectives, everywhere_sum(): got = lax.all_to_all(lay_out(grads, classes), axes, 0, 0, tiled=True)  24 us
    unnamed x39, local copies, waits for them, and re-layouts  21.2 us
    pallas_call x2, Pallas kernels, pack_columns(): pl.pallas_call(body, out_shape=jax.ShapeDtypeStruct((2, channels, 128), B...  14.3 us
    all_to_all x1, waiting for transfers between devices, everywhere_sum(): lax.all_to_all(jnp.broadcast_to(row, (n,) + row.shape[1:]), axes, 0, 0, t...  12.7 us
    pallas_call x1, Pallas kernels, error_rows(): pl.pallas_call(error_body, grid=(rows // step,), in_specs=[pl.BlockSpec((...  10.4 us
    ppermute x2, starting transfers between devices, row_halo(): top = lax.ppermute(mid[mid.shape[0] - width:], 'wide', up)  8.46 us
  transfers between devices with their start and end apart: 10, of which 5 were waited for; matrix products, arithmetic and copies ran while one was open for 12% of the time, Pallas kernels for 18%

profile of v1, /device:TPU:1, one launch (start us, length us, event | category | flops | bytes accessed | tf_op | source)
XLA Modules:
  0.0 211.1 jit_solution(13203791164250576861)
XLA Ops:
  0.7 1.8 copy.142
  3.4 4.9 %collective-permute-start = (bf16[2,80,256]{2,1,0:T(8,128)(2,1)S(1)}, bf16[2,80,256]{2,1,0:T(8,128)(2,1)S(1)}, u32[]{:S(2)}, u32[]{:S(2)}) collective-permute-start(bf16[2,80,256]{2,1,0:T(8,128)(2,1)S(1)} %get-tuple-element.67), channel_id=1, source_target_pairs={{0,4},{4,8},{8,12},{12,16},{16,20},{20,24},{24,28},{28,32},{32,36}... | collective-permute-start | bytes 245768 | tf_op jit(solution)/shard_map/ppermute | solution.py:311
  8.4 1.9 collective-permute-start.1
  11.5 2.6 %collective-permute-done.1.bottom_ref = bf16[2,80,256]{2,1,0:T(8,128)(2,1)S(1)} collective-permute-done((bf16[2,80,256]{2,1,0:T(8,128)(2,1)S(1)}, bf16[2,80,256]{2,1,0:T(8,128)(2,1)S(1)}, u32[]{:S(2)}, u32[]{:S(2)}) %collective-permute-start.1) | collective-permute-done | bytes 81952 | tf_op jit(solution)/shard_map/ppermute | solution.py:312
  14.8 7.3 %pack_columns.2 = bf16[2,80,128]{2,1,0:T(8,128)(2,1)} custom-call(bf16[32,80,256]{2,1,0:T(8,128)(2,1)} %copy-done.3, bf16[2,80,256]{2,1,0:T(8,128)(2,1)} %copy-done.5, bf16[2,80,256]{2,1,0:T(8,128)(2,1)} %copy-done.6), custom_call_target="tpu_custom_call" | custom-call | tf_op jit(solution)/shard_map/pack_columns/pallas_call | solution.py:64
  22.8 3.1 %collective-permute-start.2 = (bf16[80,128]{1,0:T(8,128)(2,1)S(1)}, bf16[80,128]{1,0:T(8,128)(2,1)S(1)}, u32[]{:S(2)}, u32[]{:S(2)}) collective-permute-start(bf16[80,128]{1,0:T(8,128)(2,1)S(1)} %get-tuple-element.76), channel_id=1, source_target_pairs={{0,1},{1,2},{2,3},{4,5},{5,6},{6,7},{8,9},{9,10},{10,11},{12,13},{... | collective-permute-start | bytes 61448 | tf_op jit(solution)/shard_map/ppermute | solution.py:318
  25.9 1.3 collective-permute-start.3
  27.2 3.0 %convolution_convert_fusion = bf16[64,8192]{1,0:T(8,128)(2,1)S(1)} fusion(pred[64,256]{1,0:T(32,128)(4,1)S(1)} %reshape.269, bf16[256,8192]{1,0:T(8,128)(2,1)} %param.10), kind=kOutput, calls=%fused_computation | convolution fusion | flops 268959744 | bytes 5259264 | tf_op jit(solution)/shard_map/dot_general | solution.py:24
  30.4 1.5 reshape.270
  31.9 8.3 %all-to-all-start = ((bf16[32,2,8192]{2,1,0:T(2,128)(2,1)}), bf16[32,2,8192]{2,1,0:T(2,128)(2,1)S(1)}, u32[]{:S(2)}, u32[]{:S(2)}) async-start(bf16[32,2,8192]{2,1,0:T(2,128)(2,1)} %reshape.270), calls=%async_computation | async-start | bytes 2097152 | tf_op jit(solution)/shard_map/all_to_all | solution.py:397
  42.8 15.7 %copy.124 = bf16[8,128,32,256]{3,1,0,2:T(8,128)(2,1)} copy(bf16[8,128,32,256]{3,2,1,0:T(8,128)(2,1)} %param.13) | data formatting | bytes 33554432 | tf_op args[3]
  58.7 37.8 %forward.1 = (bf16[7488,384]{1,0:T(8,128)(2,1)}, f32[32,128,256]{2,1,0:T(8,128)}, f32[32,128,256]{2,1,0:T(8,128)}, bf16[32,128,256]{2,1,0:T(8,128)(2,1)}, bf16[3...) custom-call(bf16[32,80,256]{2,1,0:T(8,128)(2,1)} %copy-done.3, bf16[2,80,256]{2,1,0:T(8,128)(2,1)} %copy-done.5, ...), custom_call_target="tpu_custom_call" | custom-call | tf_op jit(solution)/shard_map/forward/pallas_call | solution.py:159
  98.2 10.4 %error_rows.1.mid_ref.refs_0_ = bf16[32,64,256]{2,1,0:T(8,128)(2,1)} custom-call(bf16[64,1024]{1,0:T(8,128)(2,1)} %bitcast.96, bf16[32,1024,256]{2,1,0:T(8,128)(2,1)} %bitcast.89, f32[32,64,256]{2,1,0:T(8,128)} %get-tuple-element.20.total_ref), custom_call_target="tpu_custom_call" | custom-call | tf_op jit(solution)/shard_map/error_rows/pallas_call | solution.py:187
  109.4 3.5 %collective-permute-start.4 = (bf16[1,64,256]{2,1,0:T(8,128)(2,1)S(1)}, bf16[1,64,256]{2,1,0:T(8,128)(2,1)S(1)}, u32[]{:S(2)}, u32[]{:S(2)}) collective-permute-start(bf16[1,64,256]{2,1,0:T(8,128)(2,1)S(1)} %get-tuple-element.69), channel_id=1, source_target_pairs={{0,4},{4,8},{8,12},{12,16},{16,20},{20,24},{24,28},{28,32},{32,36}... | collective-permute-start | bytes 98312 | tf_op jit(solution)/shard_map/ppermute | solution.py:311
  113.0 1.9 collective-permute-start.5
  114.9 3.3 %collective-permute-done.5.bottom_ref.refs_2_ = bf16[1,64,256]{2,1,0:T(8,128)(2,1)S(1)} collective-permute-done((bf16[1,64,256]{2,1,0:T(8,128)(2,1)S(1)}, bf16[1,64,256]{2,1,0:T(8,128)(2,1)S(1)}, u32[]{:S(2)}, u32[]{:S(2)}) %collective-permute-start.5) | collective-permute-done | bytes 32800 | tf_op jit(solution)/shard_map/ppermute | solution.py:312
  118.8 7.0 %pack_columns.3 = bf16[2,64,128]{2,1,0:T(8,128)(2,1)} custom-call(bf16[32,64,256]{2,1,0:T(8,128)(2,1)} %error_rows.1.mid_ref.refs_0_, bf16[1,64,256]{2,1,0:T(8,128)(2,1)} %copy-done.8, bf16[1,64,256]{2,1,0:T(8,128)(2,1)} %copy-done.9), custom_call_target="tpu_custom_call" | custom-call | tf_op jit(solution)/shard_map/pack_columns/pallas_call | solution.py:64
  126.5 3.9 %collective-permute-start.6 = (bf16[64,128]{1,0:T(8,128)(2,1)S(1)}, bf16[64,128]{1,0:T(8,128)(2,1)S(1)}, u32[]{:S(2)}, u32[]{:S(2)}) collective-permute-start(bf16[64,128]{1,0:T(8,128)(2,1)S(1)} %get-tuple-element.80), channel_id=1, source_target_pairs={{0,1},{1,2},{2,3},{4,5},{5,6},{6,7},{8,9},{9,10},{10,11},{12,13},{... | collective-permute-start | bytes 49160 | tf_op jit(solution)/shard_map/ppermute | solution.py:318
  133.3 1.6 collective-permute-done.7.refs_4_
  135.5 25.7 %backward.1 = (f32[128,576]{1,0:T(8,128)}, f32[128,576]{1,0:T(8,128)}, f32[16,512]{1,0:T(8,128)}) custom-call(bf16[32,64,256]{2,1,0:T(8,128)(2,1)} %error_rows.1.mid_ref.refs_0_, bf16[1,64,256]{2,1,0:T(8,128)(2,1)} %copy-done.8, bf16[1,64,256]{2,1,0:T(8,128)(2,1)} %copy-done.9, bf16[64,128]{1,0:T(8,128)(2,1)} %copy-done.12, bf16[64,128]{1,0:T(8,128)(2,1)} %copy-done.13, ...), custom_call_target="tpu_custom_call" | custom-call | tf_op jit(solution)/shard_map/backward/pallas_call | solution.py:282
  165.2 24.0 %all_to_all.15 = bf16[128,10,128]{2,1,0:T(8,128)(2,1)S(1)} all-to-all(bf16[128,10,128]{2,1,0:T(8,128)(2,1)S(1)} %copy.134), channel_id=1, replica_groups=mesh['wide'=32,'narrow'=4] {'wide','narrow'}, dimensions={0} | all-to-all | bytes 655360 | tf_op jit(solution)/shard_map/all_to_all | solution.py:347
  190.5 3.6 %all-to-all-start.2 = ((bf16[128,10,128]{2,1,0:T(8,128)(2,1)}), bf16[128,10,128]{2,1,0:T(8,128)(2,1)S(1)}, u32[]{:S(2)}, u32[]{:S(2)}) async-start(bf16[128,10,128]{2,1,0:T(8,128)(2,1)} %broadcast_in_dim.8), calls=%async_computation.2 | async-start | bytes 1048576 | tf_op jit(solution)/shard_map/all_to_all | solution.py:353
  194.1 1.6 copy.137
  195.7 12.7 %all-to-all-done.2 = bf16[128,10,128]{2,1,0:T(8,128)(2,1)S(1)} async-done(((bf16[128,10,128]{2,1,0:T(8,128)(2,1)}), bf16[128,10,128]{2,1,0:T(8,128)(2,1)S(1)}, u32[]{:S(2)}, u32[]{:S(2)}) %all-to-all-start.2) | async-done | bytes 327712 | tf_op jit(solution)/shard_map/all_to_all | solution.py:353
  (113 shorter events, 21.5 us)
Async XLA Ops:
  0.6 9.7 %copy-start = (s32[32,4]{0,1:T(4,128)S(1)}, s32[32,4]{0,1:T(4,128)}, u32[]{:S(2)}) copy-start(s32[32,4]{0,1:T(4,128)} %param.12) | copy-start | bytes 1540
  0.6 9.7 %copy-start.14 = (s32[32,4,8]{0,2,1:T(8,128)S(1)}, s32[32,4,8]{0,2,1:T(8,128)}, u32[]{:S(2)}) copy-start(s32[32,4,8]{0,2,1:T(8,128)} %param.11) | copy-start | bytes 12292
  3.4 10.7 %copy-start.3 = (bf16[32,80,256]{2,1,0:T(8,128)(2,1)}, bf16[32,80,256]{2,1,0:T(8,128)(2,1)S(1)}, u32[]{:S(2)}) copy-start(bf16[32,80,256]{2,1,0:T(8,128)(2,1)S(1)} %fusion.1.mid_ref) | copy-start | bytes 3932164
  3.4 8.1 %collective-permute-start = (bf16[2,80,256]{2,1,0:T(8,128)(2,1)S(1)}, bf16[2,80,256]{2,1,0:T(8,128)(2,1)S(1)}, u32[]{:S(2)}, u32[]{:S(2)}) collective-permute-start(bf16[2,80,256]{2,1,0:T(8,128)(2,1)S(1)} %get-tuple-element.67), channel_id=1, source_target_pairs={{0,4},{4,8},{8,12},{12,16},{16,20},{20,24},{24,28},{28,32},{32,36}... | collective-permute-start | bytes 245768 | tf_op jit(solution)/shard_map/ppermute | solution.py:311
  8.4 5.8 %collective-permute-start.1 = (bf16[2,80,256]{2,1,0:T(8,128)(2,1)S(1)}, bf16[2,80,256]{2,1,0:T(8,128)(2,1)S(1)}, u32[]{:S(2)}, u32[]{:S(2)}) collective-permute-start(bf16[2,80,256]{2,1,0:T(8,128)(2,1)S(1)} %get-tuple-element.66), channel_id=1, source_target_pairs={{4,0},{8,4},{12,8},{16,12},{20,16},{24,20},{28,24},{32,28},{36,32}... | collective-permute-start | bytes 245768 | tf_op jit(solution)/shard_map/ppermute | solution.py:312
  11.5 2.6 %copy-start.5 = (bf16[2,80,256]{2,1,0:T(8,128)(2,1)}, bf16[2,80,256]{2,1,0:T(8,128)(2,1)S(1)}, u32[]{:S(2)}) copy-start(bf16[2,80,256]{2,1,0:T(8,128)(2,1)S(1)} %collective-permute-done.top_ref) | copy-start | bytes 245764
  22.8 7.5 %collective-permute-start.2 = (bf16[80,128]{1,0:T(8,128)(2,1)S(1)}, bf16[80,128]{1,0:T(8,128)(2,1)S(1)}, u32[]{:S(2)}, u32[]{:S(2)}) collective-permute-start(bf16[80,128]{1,0:T(8,128)(2,1)S(1)} %get-tuple-element.76), channel_id=1, source_target_pairs={{0,1},{1,2},{2,3},{4,5},{5,6},{6,7},{8,9},{9,10},{10,11},{12,13},{... | collective-permute-start | bytes 61448 | tf_op jit(solution)/shard_map/ppermute | solution.py:318
  25.9 4.5 %collective-permute-start.3 = (bf16[80,128]{1,0:T(8,128)(2,1)S(1)}, bf16[80,128]{1,0:T(8,128)(2,1)S(1)}, u32[]{:S(2)}, u32[]{:S(2)}) collective-permute-start(bf16[80,128]{1,0:T(8,128)(2,1)S(1)} %get-tuple-element.75), channel_id=1, source_target_pairs={{1,0},{2,1},{3,2},{5,4},{6,5},{7,6},{9,8},{10,9},{11,10},{13,12},{... | collective-permute-start | bytes 61448 | tf_op jit(solution)/shard_map/ppermute | solution.py:319
  30.3 10.0 %copy-start.15 = (f32[16,128]{1,0:T(8,128)S(1)}, f32[16,128]{1,0:T(8,128)}, u32[]{:S(2)}) copy-start(f32[16,128]{1,0:T(8,128)} %param.18) | copy-start | bytes 24580
  30.3 10.0 %copy-start.16 = (f32[16,128]{1,0:T(8,128)S(1)}, f32[16,128]{1,0:T(8,128)}, u32[]{:S(2)}) copy-start(f32[16,128]{1,0:T(8,128)} %param.19) | copy-start | bytes 24580
  30.3 10.8 %copy-start.4 = (bf16[64,128,3,3]{1,0,3,2:T(8,128)(2,1)S(1)}, bf16[64,128,3,3]{1,0,3,2:T(8,128)(2,1)}, u32[]{:S(2)}) copy-start(bf16[64,128,3,3]{1,0,3,2:T(8,128)(2,1)} %param.17) | copy-start | bytes 442372
  30.3 11.7 %copy-start.7 = (bf16[128,64,3,3]{0,1,3,2:T(8,128)(2,1)S(1)}, bf16[128,64,3,3]{0,1,3,2:T(8,128)(2,1)}, u32[]{:S(2)}) copy-start(bf16[128,64,3,3]{0,1,3,2:T(8,128)(2,1)} %param.16) | copy-start | bytes 442372
  30.3 12.5 %copy-start.10 = (bf16[80,128]{1,0:T(8,128)(2,1)}, bf16[80,128]{1,0:T(8,128)(2,1)S(1)}, u32[]{:S(2)}) copy-start(bf16[80,128]{1,0:T(8,128)(2,1)S(1)} %collective-permute-done.2.left_ref) | copy-start | bytes 61444
  30.4 12.4 %copy-start.11 = (bf16[80,128]{1,0:T(8,128)(2,1)}, bf16[80,128]{1,0:T(8,128)(2,1)S(1)}, u32[]{:S(2)}) copy-start(bf16[80,128]{1,0:T(8,128)(2,1)S(1)} %collective-permute-done.3.right_ref) | copy-start | bytes 61444
  31.9 64.5 %all-to-all-start = ((bf16[32,2,8192]{2,1,0:T(2,128)(2,1)}), bf16[32,2,8192]{2,1,0:T(2,128)(2,1)S(1)}, u32[]{:S(2)}, u32[]{:S(2)}) async-start(bf16[32,2,8192]{2,1,0:T(2,128)(2,1)} %reshape.270), calls=%async_computation | async-start | bytes 2097152 | tf_op jit(solution)/shard_map/all_to_all | solution.py:397
  109.4 5.5 %collective-permute-start.4 = (bf16[1,64,256]{2,1,0:T(8,128)(2,1)S(1)}, bf16[1,64,256]{2,1,0:T(8,128)(2,1)S(1)}, u32[]{:S(2)}, u32[]{:S(2)}) collective-permute-start(bf16[1,64,256]{2,1,0:T(8,128)(2,1)S(1)} %get-tuple-element.69), channel_id=1, source_target_pairs={{0,4},{4,8},{8,12},{12,16},{16,20},{20,24},{24,28},{28,32},{32,36}... | collective-permute-start | bytes 98312 | tf_op jit(solution)/shard_map/ppermute | solution.py:311
  113.0 5.2 %collective-permute-start.5 = (bf16[1,64,256]{2,1,0:T(8,128)(2,1)S(1)}, bf16[1,64,256]{2,1,0:T(8,128)(2,1)S(1)}, u32[]{:S(2)}, u32[]{:S(2)}) collective-permute-start(bf16[1,64,256]{2,1,0:T(8,128)(2,1)S(1)} %get-tuple-element.68), channel_id=1, source_target_pairs={{4,0},{8,4},{12,8},{16,12},{20,16},{24,20},{28,24},{32,28},{36,32}... | collective-permute-start | bytes 98312 | tf_op jit(solution)/shard_map/ppermute | solution.py:312
  114.9 3.3 %copy-start.8 = (bf16[1,64,256]{2,1,0:T(8,128)(2,1)}, bf16[1,64,256]{2,1,0:T(8,128)(2,1)S(1)}, u32[]{:S(2)}) copy-start(bf16[1,64,256]{2,1,0:T(8,128)(2,1)S(1)} %collective-permute-done.4.top_ref.refs_1_) | copy-start | bytes 98308
  126.5 6.8 %collective-permute-start.6 = (bf16[64,128]{1,0:T(8,128)(2,1)S(1)}, bf16[64,128]{1,0:T(8,128)(2,1)S(1)}, u32[]{:S(2)}, u32[]{:S(2)}) collective-permute-start(bf16[64,128]{1,0:T(8,128)(2,1)S(1)} %get-tuple-element.80), channel_id=1, source_target_pairs={{0,1},{1,2},{2,3},{4,5},{5,6},{6,7},{8,9},{9,10},{10,11},{12,13},{... | collective-permute-start | bytes 49160 | tf_op jit(solution)/shard_map/ppermute | solution.py:318
  130.5 4.5 %collective-permute-start.7 = (bf16[64,128]{1,0:T(8,128)(2,1)S(1)}, bf16[64,128]{1,0:T(8,128)(2,1)S(1)}, u32[]{:S(2)}, u32[]{:S(2)}) collective-permute-start(bf16[64,128]{1,0:T(8,128)(2,1)S(1)} %get-tuple-element.79), channel_id=1, source_target_pairs={{1,0},{2,1},{3,2},{5,4},{6,5},{7,6},{9,8},{10,9},{11,10},{13,12},{... | collective-permute-start | bytes 49160 | tf_op jit(solution)/shard_map/ppermute | solution.py:319
  133.3 1.6 copy-start.12
  164.5 29.7 %copy-start.2 = (bf16[32,64,256]{2,1,0:T(8,128)(2,1)S(1)}, bf16[32,64,256]{2,1,0:T(8,128)(2,1)}, u32[]{:S(2)}) copy-start(bf16[32,64,256]{2,1,0:T(8,128)(2,1)} %error_rows.1.mid_ref.refs_0_) | copy-start | bytes 3145732
  190.5 17.9 %all-to-all-start.2 = ((bf16[128,10,128]{2,1,0:T(8,128)(2,1)}), bf16[128,10,128]{2,1,0:T(8,128)(2,1)S(1)}, u32[]{:S(2)}, u32[]{:S(2)}) async-start(bf16[128,10,128]{2,1,0:T(8,128)(2,1)} %broadcast_in_dim.8), calls=%async_computation.2 | async-start | bytes 1048576 | tf_op jit(solution)/shard_map/all_to_all | solution.py:353
  194.1 17.0 %copy-start.1 = (s32[32,4]{0,1:T(4,128)S(1)}, s32[32,4]{0,1:T(4,128)}, u32[]{:S(2)}) copy-start(s32[32,4]{0,1:T(4,128)} %param.12) | copy-start | bytes 1540
  (3 other events, 1.8 us)

commit v2 on v1

v2 whole, which is shorter than its diff:
```python
import jax
import jax.numpy as jnp
from jax import lax
from jax.experimental import pallas as pl
from jax.experimental.pallas import tpu as pltpu
from jax.sharding import PartitionSpec as P

F32 = jnp.float32
BF16 = jnp.bfloat16
CX = 80


def whole():
    return pl.BlockSpec(memory_space=pltpu.VMEM)


def nt(a, b):
    return lax.dot_general(a, b, (((1,), (1,)), ((), ())), preferred_element_type=F32)


def dot(a, b):
    return jnp.dot(a, b, preferred_element_type=F32)


def iota(shape, dim):
    return lax.broadcasted_iota(jnp.int32, shape, dim)


def in_hbm(*arrays):
    return [pltpu.with_memory_space_constraint(a, pltpu.HBM) for a in arrays]


def params(mebibytes):
    return pltpu.CompilerParams(vmem_limit_bytes=mebibytes * 1024 * 1024)


def pack_columns(mid, top, bottom, width):
    rows, channels, cols = mid.shape
    span = 128 // width
    group = 8

    def body(mid_ref, top_ref, bottom_ref, out_ref):
        q = iota((cols, 256), 0)
        lane = iota((cols, 256), 1)
        part = (lane % 128) // span
        source = jnp.where(lane < 128, part, cols - width + part)
        base = jnp.where(q == source, 1.0, 0.0).astype(BF16)
        place = iota((channels, 256), 1) % span
        acc = jnp.zeros((channels, 256), F32)

        def put(acc, row, value):
            count = value.shape[0]
            picked = dot(value.reshape(count * channels, cols), base)
            for k in range(count):
                acc = jnp.where(place == row + k, picked[k * channels : (k + 1) * channels], acc)
            return acc

        acc = put(acc, 0, top_ref[...])
        acc = put(acc, width + rows, bottom_ref[...])
        for g in range(rows // group):
            acc = put(acc, width + g * group, mid_ref[pl.ds(g * group, group)])
        out_ref[0] = acc[:, :128].astype(BF16)
        out_ref[1] = acc[:, 128:].astype(BF16)

    return pl.pallas_call(
        body,
        out_shape=jax.ShapeDtypeStruct((2, channels, 128), BF16),
        in_specs=[whole()] * 3,
        out_specs=whole(),
        compiler_params=params(16),
        name="pack_columns",
    )(mid, top, bottom)


def shifted(data, halo, row):
    lane = iota(data.shape, 1)
    before = pltpu.roll(halo, (128 - row) % 128, 1)
    after = pltpu.roll(halo, (191 - row) % 128, 1)
    left = jnp.where(lane == 0, jnp.concatenate([before, before], axis=1), pltpu.roll(data, 1, 1))
    right = jnp.where(lane == 255, jnp.concatenate([after, after], axis=1), pltpu.roll(data, 255, 1))
    return left, right


XS_ROW = 208


def table_split(table):
    high = table.astype(BF16).astype(F32)
    middle = (table - high).astype(BF16).astype(F32)
    low = table - high - middle
    lane = iota(table.shape, 1)
    return jnp.where(lane < 16, high, jnp.where(lane < 32, middle, low)).astype(BF16)


def onehot_of(terrain):
    cls = jnp.broadcast_to(terrain, (16, terrain.shape[1]))
    return jnp.where(cls == (iota(cls.shape, 0) + 1).astype(F32), 1.0, 0.0).astype(BF16)


STEP = 4


def prepare_forward(
    mid_ref, top_ref, bottom_ref, own_ref, left_ref, right_ref, w1_ref, gs_ref, xs_ref, split_ref, halo_ref
):
    rows = mid_ref.shape[0]
    low_half = iota((CX, 128), 1) < 64
    left, right = left_ref[...].astype(F32), right_ref[...].astype(F32)
    own_left, own_right = own_ref[0].astype(F32), own_ref[1].astype(F32)
    near0 = jnp.where(low_half, left, own_right)
    near1 = jnp.where(low_half, pltpu.roll(left, 64, 1), pltpu.roll(right, 64, 1))
    near2 = jnp.where(low_half, own_left, right)
    halo_ref[0] = near1[:64].astype(BF16)
    halo_in = halo_ref[0]

    def build(rows_of):
        done = []
        for row, own in rows_of:
            data = own[:64]
            terrain = own[64:80].astype(F32)[0:1]
            before, after = shifted(data, halo_in, row)
            done.append((row, before, data, after, onehot_of(terrain)))
        for row, before, data, after, hot in done:
            at = row * XS_ROW if isinstance(row, int) else pl.multiple_of(row * XS_ROW, 16)
            xs_ref[pl.ds(at, 64), :] = before
            xs_ref[pl.ds(at + 64, 64), :] = data
            xs_ref[pl.ds(at + 128, 64), :] = after
            xs_ref[pl.ds(at + 192, 16), :] = hot

    build([(k, top_ref[k]) for k in range(2)] + [(rows + 2 + k, bottom_ref[k]) for k in range(2)])

    def build_mid(i, carry):
        build([(i * 4 + k + 2, mid_ref[i * 4 + k]) for k in range(4)])
        return carry

    lax.fori_loop(0, rows // 4, build_mid, 0)

    split_ref[...] = table_split(gs_ref[...])
    columns = []
    for a in range(3):
        for near in (near0, near1, near2):
            columns.append(pltpu.roll(near[:64], (128 - a) % 128, 1).astype(BF16))
    side_first = dot(w1_ref[...], jnp.concatenate(columns, axis=0))
    side_hot = onehot_of(pltpu.roll(near1[64:80], 127, 1)[0:1])
    side_pre, side_sigma = activation(split_ref[...], side_first, side_hot)
    hs_halo = (side_pre * side_sigma).astype(BF16)
    halo_ref[1] = hs_halo[:64]
    halo_ref[2] = hs_halo[64:]


def activation(split, first, hot):
    table = dot(split, jnp.concatenate([hot, hot, hot], axis=0))
    gain, shift = table[:128], table[128:]
    pre = first * gain + shift
    sigma = 1.0 / (1.0 + jnp.exp(-pre))
    return pre, sigma


def forward_body(
    mid_ref, top_ref, bottom_ref, own_ref, left_ref, right_ref, w1_ref, gs_ref, w2_ref,
    xs_out, first_ref, slope_ref, hidden_ref, onehot_ref, total_ref, xs_ref, hs_ref, split_ref, halo_ref,
):
    rows = mid_ref.shape[0]
    step = pl.program_id(0)

    @pl.when(step == 0)
    def _():
        prepare_forward(
            mid_ref, top_ref, bottom_ref, own_ref, left_ref, right_ref, w1_ref, gs_ref, xs_ref, split_ref, halo_ref
        )

    block = STEP * XS_ROW
    xs_out[...] = xs_ref[pl.ds(pl.multiple_of(step * block, 16), block), :]

    def activate(hs, keep):
        done = []
        split = split_ref[...]
        hidden_halo = jnp.concatenate([halo_ref[1], halo_ref[2]], axis=0)
        for h in hs:
            at = [(h + a) * XS_ROW for a in range(3)]
            if not isinstance(h, int):
                at = [pl.multiple_of(x, 16) for x in at]
            pieces = [xs_ref[pl.ds(x, 192), :] for x in at]
            first = dot(w1_ref[...], jnp.concatenate(pieces, axis=0))
            hot = xs_ref[pl.ds(at[1] + 192, 16), :]
            pre, sigma = activation(split, first, hot)
            center = (pre * sigma).astype(BF16)
            before, after = shifted(center, hidden_halo, h)
            slope = sigma * (1.0 + pre * (1.0 - sigma)) if keep else None
            done.append((h, first, slope, before, center, after, hot))
        for k, (h, first, slope, before, center, after, hot) in enumerate(done):
            at = h * 384 if isinstance(h, int) else pl.multiple_of(h * 384, 16)
            hs_ref[pl.ds(at, 128), :] = before
            hs_ref[pl.ds(at + 128, 128), :] = center
            hs_ref[pl.ds(at + 256, 128), :] = after
            if keep:
                first_ref[k] = first
                slope_ref[k] = slope
                hidden_ref[k] = center
                onehot_ref[k] = hot

    @pl.when(step == 0)
    def _():
        activate([0, rows + 1], False)

    @pl.when(step < rows // STEP)
    def _():
        activate([step * STEP + k + 1 for k in range(STEP)], True)

    @pl.when(step > 0)
    def _():
        sums = []
        for k in range(STEP):
            r = (step - 1) * STEP + k
            stack = hs_ref[pl.ds(pl.multiple_of(r * 384, 16), 1152), :]
            sums.append(dot(w2_ref[...], stack) + mid_ref[r][:64].astype(F32))
        for k in range(STEP):
            total_ref[k] = sums[k]


def forward(mid, top, bottom, own, left, right, w1, gs, w2):
    rows = mid.shape[0]
    last = rows // STEP - 1

    def block(shape):
        return pl.BlockSpec((STEP,) + shape, lambda i: (jnp.minimum(i, last), 0, 0))

    return pl.pallas_call(
        forward_body,
        grid=(rows // STEP + 1,),
        out_shape=(
            pltpu.HBM(((rows + 4) * XS_ROW, 256), BF16),
            pltpu.HBM((rows, 128, 256), F32),
            pltpu.HBM((rows, 128, 256), F32),
            pltpu.HBM((rows, 128, 256), BF16),
            pltpu.HBM((rows, 16, 256), BF16),
            pltpu.HBM((rows, 64, 256), F32),
        ),
        in_specs=[whole()] * 9,
        out_specs=(
            pl.BlockSpec((STEP * XS_ROW, 256), lambda i: (i, 0)),
            block((128, 256)), block((128, 256)), block((128, 256)), block((16, 256)),
            pl.BlockSpec((STEP, 64, 256), lambda i: (jnp.maximum(i - 1, 0), 0, 0)),
        ),
        scratch_shapes=[
            pltpu.VMEM(((rows + 4) * XS_ROW, 256), BF16),
            pltpu.VMEM(((rows + 2) * 384, 256), BF16),
            pltpu.VMEM((256, 48), BF16),
            pltpu.VMEM((3, 64, 128), BF16),
        ],
        compiler_params=params(28),
        name="forward",
    )(mid, top, bottom, own, left, right, w1, gs, w2)


def rows_first(weights, start, stop):
    rows, cols = weights.shape[1:]
    chunk = 128

    def body(in_ref, out_ref):
        out_ref[...] = jnp.swapaxes(in_ref[...], 0, 1)

    return pl.pallas_call(
        body,
        grid=((stop - start) // chunk,),
        in_specs=[pl.BlockSpec((chunk, rows, cols), lambda i: (i + start // chunk, 0, 0))],
        out_specs=pl.BlockSpec((rows, chunk, cols), lambda i: (0, i, 0)),
        out_shape=pltpu.HBM((rows, stop - start, cols), BF16),
        compiler_params=params(14),
        name="rows_first",
    )(*in_hbm(weights))


def error_rows(blocks, weights, total):
    rows, channels, cols = total.shape
    step = 8

    def body(blocks_ref, *refs):
        parts, total_ref, error_ref = refs[:-2], refs[-2], refs[-1]
        for k in range(step):
            value = total_ref[k]
            at = 0
            for part in parts:
                depth = part.shape[1]
                value -= dot(blocks_ref[:, at : at + depth], part[k])
                at += depth
            error_ref[k] = value.astype(BF16)

    return pl.pallas_call(
        body,
        grid=(rows // step,),
        in_specs=[pl.BlockSpec(blocks.shape, lambda i: (0, 0))]
        + [pl.BlockSpec((step,) + w.shape[1:], lambda i: (i, 0, 0)) for w in weights]
        + [pl.BlockSpec((step, channels, cols), lambda i: (i, 0, 0))],
        out_specs=pl.BlockSpec((step, channels, cols), lambda i: (i, 0, 0)),
        out_shape=jax.ShapeDtypeStruct((rows, channels, cols), BF16),
        compiler_params=params(20),
        name="error_rows",
    )(blocks, *in_hbm(*weights, total))


def backward_body(
    scale, err_ref, top_ref, bottom_ref, left_ref, right_ref, xs_ref, xs_next, first_ref, slope_ref,
    hidden_ref, onehot_ref, wb_ref, gain_ref, grads_ref, row_ref, es_ref, g1_ref, g2_ref, cls_ref, split_ref,
):
    rows = err_ref.shape[0]
    step = pl.program_id(0)

    @pl.when(step == 0)
    def _():
        left, right = left_ref[...].astype(F32), right_ref[...].astype(F32)
        halo = jnp.where(iota(left.shape, 1) < 64, left, pltpu.roll(right, 64, 1)).astype(BF16)

        def build(rows_of):
            done = [(row, own, shifted(own, halo, row)) for row, own in rows_of]
            for row, own, (before, after) in done:
                at = row * 192
                es_ref[pl.ds(at, 64), :] = before
                es_ref[pl.ds(at + 64, 64), :] = own
                es_ref[pl.ds(at + 128, 64), :] = after

        build([(0, top_ref[0]), (rows + 1, bottom_ref[0])])
        for r in range(0, rows, 4):
            build([(r + k + 1, err_ref[r + k]) for k in range(4)])
        g1_ref[...] = jnp.zeros_like(g1_ref)
        g2_ref[...] = jnp.zeros_like(g2_ref)
        cls_ref[...] = jnp.zeros_like(cls_ref)
        split_ref[...] = table_split(gain_ref[...])

    split = split_ref[...]
    stacks, acts, inputs, classes = [], [], [], []
    for k in range(STEP):
        r = step * STEP + k
        stack = es_ref[pl.ds(pl.multiple_of(r * 192, 16), 576), :]
        back = dot(wb_ref[...], stack)
        delta = back * slope_ref[k] * scale
        hot = onehot_ref[k]
        gain = dot(split, jnp.concatenate([hot, hot, hot], axis=0))
        acts.append((delta * gain).astype(BF16))
        scaled_first = delta * first_ref[k]
        d_high = delta.astype(BF16)
        d_low = (delta - d_high.astype(F32)).astype(BF16)
        f_high = scaled_first.astype(BF16)
        f_low = (scaled_first - f_high.astype(F32)).astype(BF16)
        classes.append(jnp.concatenate([d_high, d_low, f_high, f_low], axis=0))
        pieces = []
        for x in range(k + 1, k + 4):
            ref, at = (xs_ref, x) if x < STEP else (xs_next, x - STEP)
            pieces.append(ref[pl.ds(at * XS_ROW, 192), :])
        inputs.append(jnp.concatenate(pieces, axis=0))
        stacks.append(stack)

    def across(parts):
        return jnp.concatenate(parts, axis=1)

    hots = across([onehot_ref[k] for k in range(STEP)])
    acc1 = g1_ref[...] + nt(across(inputs), across(acts))
    acc2 = g2_ref[...] + nt(across(stacks), across([hidden_ref[k] for k in range(STEP)]))
    acc3 = cls_ref[...] + nt(hots, across(classes))
    g1_ref[...] = acc1
    g2_ref[...] = acc2
    cls_ref[...] = acc3

    @pl.when(step == pl.num_programs(0) - 1)
    def _():
        grads_ref[pl.ds(0, 576), :] = acc1.astype(BF16)
        grads_ref[pl.ds(576, 576), :] = (acc2 * scale).astype(BF16)
        sums = jnp.concatenate([acc3[:, :128] + acc3[:, 128:256], acc3[:, 256:384] + acc3[:, 384:]], axis=1)
        high = sums.astype(BF16)
        middle = (sums - high.astype(F32)).astype(BF16)
        low = (sums - high.astype(F32) - middle.astype(F32)).astype(BF16)
        repeat = jnp.where(iota((128, 16), 0) // 8 == iota((128, 16), 1), 1.0, 0.0).astype(BF16)
        own = iota((128, 256), 1) // 32 == iota((128, 256), 0) % 8
        row = jnp.zeros((128, 128), F32)
        for part, value in enumerate((high, middle, low)):
            fold = jnp.where(iota((256, 128), 0) % 32 + 32 * part == iota((256, 128), 1), 1.0, 0.0)
            row += dot(jnp.where(own, dot(repeat, value), 0.0).astype(BF16), fold.astype(BF16))
        row_ref[...] = row.astype(BF16)


def backward(scale, err, top, bottom, left, right, xs, first, slope, hidden, onehot, wb, gains):
    rows = err.shape[0]

    def const(shape):
        return pl.BlockSpec(shape, lambda i: (0,) * len(shape))

    def moving(shape):
        return pl.BlockSpec((STEP,) + shape[1:], lambda i: (i, 0, 0))

    def body(*refs):
        backward_body(scale, *refs)

    return pl.pallas_call(
        body,
        grid=(rows // STEP,),
        in_specs=[
            const(err.shape), const(top.shape), const(bottom.shape), const(left.shape), const(right.shape),
            pl.BlockSpec((STEP * XS_ROW, 256), lambda i: (i, 0)),
            pl.BlockSpec((STEP * XS_ROW, 256), lambda i: (i + 1, 0)), moving(first.shape), moving(slope.shape), moving(hidden.shape),
            moving(onehot.shape), const(wb.shape), const(gains.shape),
        ],
        out_specs=(const((1152, 128)), const((128, 128))),
        out_shape=(jax.ShapeDtypeStruct((1152, 128), BF16), jax.ShapeDtypeStruct((128, 128), BF16)),
        scratch_shapes=[
            pltpu.VMEM(((rows + 2) * 192, 256), BF16),
            pltpu.VMEM((576, 128), F32),
            pltpu.VMEM((576, 128), F32),
            pltpu.VMEM((16, 512), F32),
            pltpu.VMEM((128, 48), BF16),
        ],
        compiler_params=params(32),
        name="backward",
    )(err, top, bottom, left, right, *in_hbm(xs, xs, first, slope, hidden, onehot), wb, gains)


def shifts(axis):
    size = lax.axis_size(axis)
    up = [(i, i + 1) for i in range(size - 1)]
    down = [(i + 1, i) for i in range(size - 1)]
    return up, down


def row_halo(mid, width):
    up, down = shifts("wide")
    top = lax.ppermute(mid[mid.shape[0] - width :], "wide", up)
    bottom = lax.ppermute(mid[:width], "wide", down)
    return top, bottom


def column_halo(packed):
    up, down = shifts("narrow")
    left = lax.ppermute(packed[1], "narrow", up)
    right = lax.ppermute(packed[0], "narrow", down)
    return left, right


def split3(value):
    high = lax.reduce_precision(value, 8, 7)
    middle = lax.reduce_precision(value - high, 8, 7)
    low = value - high - middle
    return high.astype(BF16), middle.astype(BF16), low.astype(BF16)


def everywhere_sum(grads, parts):
    axes = ("wide", "narrow")
    n = lax.axis_size(axes)
    per = grads.shape[0] // n
    rest = parts.reshape(n, -1, 128)
    table = jnp.concatenate([grads.reshape(n, per, 128), rest], axis=1)
    got = lax.all_to_all(table, axes, 0, 0, tiled=True)
    total = got.astype(F32).sum(0)
    small = total[per:].reshape(-1, 4, 32)
    high, middle, low = split3(small.sum(1))
    small = jnp.stack([high, middle, low, jnp.zeros_like(low)], axis=1).reshape(-1, 128)
    row = jnp.concatenate([total[:per].astype(BF16), small], axis=0)
    spread = lax.all_to_all(jnp.broadcast_to(row, (n,) + row.shape), axes, 0, 0, tiled=True)
    grads = spread[:, :per].reshape(grads.shape).astype(F32)
    small = spread[:, per:].astype(F32).reshape(128, 4, 32).sum(1)
    return grads, small.reshape(16, 256)


def shards(
    teacher,
    intersection_ids,
    slot_counts,
    intersection_weights,
    student_input,
    terrain_class,
    conv_first,
    conv_second,
    class_gain,
    class_shift,
):
    band = lax.axis_index("wide")
    column = lax.axis_index("narrow")
    n_bands = lax.axis_size("wide")
    held = teacher.shape[0]
    slots = intersection_ids.shape[2]
    depth = intersection_weights.shape[1]
    rows, cols = student_input.shape[1:]

    terrain = (terrain_class + 1).astype(BF16)[:, None, :]
    mid = jnp.concatenate(
        [student_input.transpose(1, 0, 2), jnp.pad(terrain, ((0, 0), (0, CX - 65), (0, 0)))], axis=1
    )
    top, bottom = row_halo(mid, 2)
    weights = intersection_weights.reshape(-1, rows, cols)
    deep = weights.shape[0]
    cuts = (0, deep // 4, deep // 2, deep)
    parts = [rows_first(weights, x, y) for x, y in zip(cuts, cuts[1:])]
    top, bottom, parts[0] = lax.optimization_barrier((top, bottom, parts[0]))
    own = pack_columns(mid, top, bottom, 2)
    left, right = column_halo(own)

    ids = lax.dynamic_index_in_dim(intersection_ids, column, 1, keepdims=False)
    counts = lax.dynamic_index_in_dim(slot_counts, column, 1, keepdims=False)
    owner, local = ids // held, ids % held
    slot = lax.broadcasted_iota(jnp.int32, (n_bands, slots), 1)
    live = slot < counts[:, None]
    same = (owner[:, :, None] == owner[:, None, :]) & live[:, None, :]
    rank = (same & (slot[:1, None, :] < slot[:1, :, None])).sum(-1)
    which = lax.broadcasted_iota(jnp.int32, (n_bands, 2, slots), 1)
    mine = (live & (owner == band))[:, None, :] & (rank[:, None, :] == which)
    pick = (mine[..., None] & (local[:, None, :, None] == jnp.arange(held))).any(2)
    outgoing = dot(pick.reshape(2 * n_bands, held).astype(BF16), teacher).astype(BF16)
    outgoing, left, right, parts[1] = lax.optimization_barrier((outgoing, left, right, parts[1]))
    incoming = lax.all_to_all(
        outgoing.reshape(n_bands, 2, -1), "wide", split_axis=0, concat_axis=0, tiled=True
    )

    w1 = conv_first.transpose(0, 2, 3, 1).reshape(128, 576)
    w2 = conv_second.transpose(0, 2, 3, 1).reshape(64, 1152)
    wb = jnp.flip(conv_second, (2, 3)).transpose(1, 2, 3, 0).reshape(128, 576)
    gain3 = jnp.tile(class_gain.T, (1, 3))
    gs = jnp.concatenate([gain3, jnp.tile(class_shift.T, (1, 3))], axis=0)
    xs, first, slope, hidden, onehot, total = forward(mid, top, bottom, own, left, right, w1, gs, w2)

    my_owner = lax.dynamic_index_in_dim(owner, band, 0, keepdims=False)
    my_live = lax.dynamic_index_in_dim(live, band, 0, keepdims=False)
    my_rank = lax.dynamic_index_in_dim(rank, band, 0, keepdims=False)
    pair = lax.broadcasted_iota(jnp.int32, (slots, 2 * n_bands), 1)
    take = ((pair == (my_owner * 2 + my_rank)[:, None]) & my_live[:, None]).astype(BF16)
    blocks = dot(take, incoming.reshape(2 * n_bands, -1)).astype(BF16)
    blocks = blocks.reshape(slots * depth, -1).T

    err = error_rows(blocks, parts, total)
    error_field = err.transpose(1, 0, 2)
    e_top, e_bottom = row_halo(err, 1)
    e_left, e_right = column_halo(pack_columns(err, e_top, e_bottom, 1))
    scale = 1.0 / (rows * cols)
    grads, class_rows = backward(
        scale, err, e_top, e_bottom, e_left, e_right, xs, first, slope, hidden, onehot, wb, gain3
    )
    grads, classes = everywhere_sum(grads, class_rows)
    grad_first = grads[:576].reshape(3, 3, 64, 128).transpose(3, 2, 0, 1)
    grad_second = jnp.flip(grads[576:].reshape(3, 3, 64, 128), (0, 1)).transpose(2, 3, 0, 1)
    return (error_field, grad_first, grad_second, classes[:, 128:], classes[:, :128])


def solution(mesh):
    in_specs = (
        P("wide", None),
        P(),
        P(),
        P(None, None, "wide", "narrow"),
        P(None, "wide", "narrow"),
        P("wide", "narrow"),
        P(),
        P(),
        P(),
        P(),
    )
    out_specs = (P(None, "wide", "narrow"), P(), P(), P(), P())
    return jax.shard_map(shards, mesh=mesh, in_specs=in_specs, out_specs=out_specs, check_vma=False)
```

time: 212 us -> 148 us (0.70)
  Pallas kernels: 88.2 us -> 53.2 us
  local copies, waits for them, and re-layouts: 35.5 us -> 10.9 us
  blocking collectives: 24 us -> 0 us
  waiting for transfers between devices: 20.3 us -> 32.8 us
  starting transfers between devices: 33.9 us -> 44.8 us
  matrix products: 3.33 us -> 1.14 us
    all_to_all x1 -> x0, blocking collectives: 24 us -> none  [everywhere_sum(): got = lax.all_to_all(lay_out(grads, classes), axes, 0, 0, tiled=True)]
    pallas_call x3 -> x6, Pallas kernels: 73.9 us -> 52.1 us  [the longest x3 16.1 us: rows_first(): pl.pallas_call(body, grid=((stop - start) // chunk,), in_specs=[pl.BlockS...]
    unnamed x39 -> x19, local copies, waits for them, and re-layouts: 21.2 us -> 3.54 us
    all_to_all x1 -> x2, waiting for transfers between devices: 12.7 us -> 26.8 us  [the longest x1 14.1 us: everywhere_sum(): got = lax.all_to_all(table, axes, 0, 0, tiled=True)]
    pallas_call x2, Pallas kernels: 14.3 us -> 1.08 us  [pack_columns(): pl.pallas_call(body, out_shape=jax.ShapeDtypeStruct((2, channels, 128), B...]
    all_to_all x1 -> x2, starting transfers between devices: 3.64 us -> 13.7 us  [the longest x1 10.1 us: everywhere_sum(): got = lax.all_to_all(table, axes, 0, 0, tiled=True)]
    ppermute x2, waiting for transfers between devices: 5.91 us -> 3.3 us  [row_halo(): bottom = lax.ppermute(mid[:width], 'wide', down)]
    dot_general x2, matrix products: 3.33 us -> 1.14 us  [dot(): return jnp.dot(a, b, preferred_element_type=F32)]
  transfers between devices with their start and end apart: 10 -> 11, of which waited for: 5 -> 4; matrix products, arithmetic and copies ran while one was open for 12% -> 3% of each run, Pallas kernels for 18% -> 20%
where the time goes in v2:
time: 148 us; the launch traced here: 147 us
  Pallas kernels  53.2 us (36%)
  starting transfers between devices  44.8 us (30%)
  waiting for transfers between devices  32.8 us (22%)
  local copies, waits for them, and re-layouts  10.9 us (7%)
  other arithmetic  3.13 us (2%)
    pallas_call x3, Pallas kernels, rows_first(): pl.pallas_call(body, grid=((stop - start) // chunk,), in_specs=[pl.BlockS...  16.1 us
    pallas_call x1, Pallas kernels, backward(): pl.pallas_call(body, grid=(rows // STEP,), in_specs=[const(err.shape), co...  14.2 us
    all_to_all x1, waiting for transfers between devices, everywhere_sum(): got = lax.all_to_all(table, axes, 0, 0, tiled=True)  14.1 us
    pallas_call x1, Pallas kernels, forward(): pl.pallas_call(forward_body, grid=(rows // STEP + 1,), out_shape=(pltpu.H...  13.8 us
    all_to_all x1, waiting for transfers between devices, everywhere_sum(): lax.all_to_all(jnp.broadcast_to(row, (n,) + row.shape), axes, 0, 0, tiled...  12.7 us
    all_to_all x1, starting transfers between devices, everywhere_sum(): got = lax.all_to_all(table, axes, 0, 0, tiled=True)  10.1 us
    all_to_all x1, starting transfers between devices, shards(): lax.all_to_all(outgoing.reshape(n_bands, 2, -1), 'wide', split_axis=0, co...  8.59 us
    ppermute x2, starting transfers between devices, row_halo(): top = lax.ppermute(mid[mid.shape[0] - width:], 'wide', up)  8.47 us
  transfers between devices with their start and end apart: 11, of which 4 were waited for; matrix products, arithmetic and copies ran while one was open for 3% of the time, Pallas kernels for 20%

profile of v2, /device:TPU:1, one launch (start us, length us, event | category | flops | bytes accessed | tf_op | source)
XLA Modules:
  0.0 147.0 jit_solution(8713064868557158994)
XLA Ops:
  0.7 1.8 %copy.96 = bf16[64,32,256]{2,0,1:T(8,128)(2,1)S(1)} copy(bf16[64,32,256]{2,1,0:T(8,128)(2,1)} %param.14) | data formatting | bytes 2097152 | tf_op args[4]
  3.4 4.9 %collective-permute-start = (bf16[2,80,256]{2,1,0:T(8,128)(2,1)S(1)}, bf16[2,80,256]{2,1,0:T(8,128)(2,1)S(1)}, u32[]{:S(2)}, u32[]{:S(2)}) collective-permute-start(bf16[2,80,256]{2,1,0:T(8,128)(2,1)S(1)} %get-tuple-element.63), channel_id=1, source_target_pairs={{0,4},{4,8},{8,12},{12,16},{16,20},{20,24},{24,28},{28,32},{32,36}... | collective-permute-start | bytes 245768 | tf_op jit(solution)/shard_map/ppermute | solution.py:425
  8.4 1.9 %collective-permute-start.1 = (bf16[2,80,256]{2,1,0:T(8,128)(2,1)S(1)}, bf16[2,80,256]{2,1,0:T(8,128)(2,1)S(1)}, u32[]{:S(2)}, u32[]{:S(2)}) collective-permute-start(bf16[2,80,256]{2,1,0:T(8,128)(2,1)S(1)} %get-tuple-element.62), channel_id=1, source_target_pairs={{4,0},{8,4},{12,8},{16,12},{20,16},{24,20},{28,24},{32,28},{36,32}... | collective-permute-start | bytes 245768 | tf_op jit(solution)/shard_map/ppermute | solution.py:426
  11.5 4.2 %rows_first.3.refs_0_ = bf16[32,256,256]{2,1,0:T(8,128)(2,1)} custom-call(bf16[1024,32,256]{2,1,0:T(8,128)(2,1)} %bitcast.80), custom_call_target="tpu_custom_call" | custom-call | tf_op jit(solution)/shard_map/rows_first/pallas_call | solution.py:263
  16.4 3.1 %collective-permute-start.2 = (bf16[80,128]{1,0:T(8,128)(2,1)S(1)}, bf16[80,128]{1,0:T(8,128)(2,1)S(1)}, u32[]{:S(2)}, u32[]{:S(2)}) collective-permute-start(bf16[80,128]{1,0:T(8,128)(2,1)S(1)} %get-tuple-element.69), channel_id=1, source_target_pairs={{0,1},{1,2},{2,3},{4,5},{5,6},{6,7},{8,9},{9,10},{10,11},{12,13},{... | collective-permute-start | bytes 61448 | tf_op jit(solution)/shard_map/ppermute | solution.py:432
  19.5 1.3 collective-permute-start.3
  21.6 4.1 %rows_first.4.refs_1_ = bf16[32,256,256]{2,1,0:T(8,128)(2,1)} custom-call(bf16[1024,32,256]{2,1,0:T(8,128)(2,1)} %bitcast.81), custom_call_target="tpu_custom_call" | custom-call | tf_op jit(solution)/shard_map/rows_first/pallas_call | solution.py:263
  25.7 1.5 %reshape.278 = bf16[32,2,8192]{2,1,0:T(2,128)(2,1)} reshape(bf16[64,8192]{1,0:T(8,128)(2,1)S(1)} %convolution_convert_fusion) | data formatting | bytes 2097152 | tf_op jit(solution)/shard_map/reshape | solution.py:508
  27.2 8.6 %all-to-all-start = ((bf16[32,2,8192]{2,1,0:T(2,128)(2,1)}), bf16[32,2,8192]{2,1,0:T(2,128)(2,1)S(1)}, u32[]{:S(2)}, u32[]{:S(2)}) async-start(bf16[32,2,8192]{2,1,0:T(2,128)(2,1)} %reshape.278), calls=%async_computation | async-start | bytes 2097152 | tf_op jit(solution)/shard_map/all_to_all | solution.py:507
  35.9 7.8 %rows_first.5.refs_2_ = bf16[32,512,256]{2,1,0:T(8,128)(2,1)} custom-call(bf16[1024,32,256]{2,1,0:T(8,128)(2,1)} %bitcast.82), custom_call_target="tpu_custom_call" | custom-call | tf_op jit(solution)/shard_map/rows_first/pallas_call | solution.py:263
  44.5 13.8 %forward.1 = (bf16[7488,256]{1,0:T(8,128)(2,1)}, f32[32,128,256]{2,1,0:T(8,128)}, f32[32,128,256]{2,1,0:T(8,128)}, bf16[32,128,256]{2,1,0:T(8,128)(2,1)}, bf16[3...) custom-call(bf16[32,80,256]{2,1,0:T(8,128)(2,1)S(1)} %fusion.1.mid_ref, ...), custom_call_target="tpu_custom_call" | custom-call | tf_op jit(solution)/shard_map/forward/pallas_call | solution.py:228
  59.5 7.9 %error_rows.1.mid_ref.refs_0_ = bf16[32,64,256]{2,1,0:T(8,128)(2,1)S(1)} custom-call(bf16[64,1024]{1,0:T(8,128)(2,1)S(1)} %bitcast.78, bf16[32,256,256]{2,1,0:T(8,128)(2,1)} %rows_first.3.refs_0_, bf16[32,256,256]{2,1,0:T(8,128)(2,1)} %rows_first.4.refs_1_, bf16[32,512,256]{2,1,0:T(8,128)(2,1)} %rows_first.5.refs_2_, f32[32,64,256]{2,1,0:T(8,128)} %get-tuple-element.27.refs_3_), custom_call_target="tpu_custom_call" | custom-call | tf_op jit(solution)/shard_map/error_rows/pallas_call | solution.py:289
  67.4 3.5 %collective-permute-start.4 = (bf16[1,64,256]{2,1,0:T(8,128)(2,1)S(1)}, bf16[1,64,256]{2,1,0:T(8,128)(2,1)S(1)}, u32[]{:S(2)}, u32[]{:S(2)}) collective-permute-start(bf16[1,64,256]{2,1,0:T(8,128)(2,1)S(1)} %get-tuple-element.67), channel_id=1, source_target_pairs={{0,4},{4,8},{8,12},{12,16},{16,20},{20,24},{24,28},{28,32},{32,36}... | collective-permute-start | bytes 98312 | tf_op jit(solution)/shard_map/ppermute | solution.py:425
  70.9 1.9 %collective-permute-start.5 = (bf16[1,64,256]{2,1,0:T(8,128)(2,1)S(1)}, bf16[1,64,256]{2,1,0:T(8,128)(2,1)S(1)}, u32[]{:S(2)}, u32[]{:S(2)}) collective-permute-start(bf16[1,64,256]{2,1,0:T(8,128)(2,1)S(1)} %get-tuple-element.66), channel_id=1, source_target_pairs={{4,0},{8,4},{12,8},{16,12},{20,16},{24,20},{28,24},{32,28},{36,32}... | collective-permute-start | bytes 98312 | tf_op jit(solution)/shard_map/ppermute | solution.py:426
  72.9 3.3 %collective-permute-done.5.bottom_ref.refs_2_ = bf16[1,64,256]{2,1,0:T(8,128)(2,1)S(1)} collective-permute-done((bf16[1,64,256]{2,1,0:T(8,128)(2,1)S(1)}, bf16[1,64,256]{2,1,0:T(8,128)(2,1)S(1)}, u32[]{:S(2)}, u32[]{:S(2)}) %collective-permute-start.5) | collective-permute-done | bytes 32800 | tf_op jit(solution)/shard_map/ppermute | solution.py:426
  76.7 4.3 %collective-permute-start.6 = (bf16[64,128]{1,0:T(8,128)(2,1)S(1)}, bf16[64,128]{1,0:T(8,128)(2,1)S(1)}, u32[]{:S(2)}, u32[]{:S(2)}) collective-permute-start(bf16[64,128]{1,0:T(8,128)(2,1)S(1)} %get-tuple-element.71), channel_id=1, source_target_pairs={{0,1},{1,2},{2,3},{4,5},{5,6},{6,7},{8,9},{9,10},{10,11},{12,13},{... | collective-permute-start | bytes 49160 | tf_op jit(solution)/shard_map/ppermute | solution.py:432
  81.0 1.5 %collective-permute-start.7 = (bf16[64,128]{1,0:T(8,128)(2,1)S(1)}, bf16[64,128]{1,0:T(8,128)(2,1)S(1)}, u32[]{:S(2)}, u32[]{:S(2)}) collective-permute-start(bf16[64,128]{1,0:T(8,128)(2,1)S(1)} %get-tuple-element.70), channel_id=1, source_target_pairs={{1,0},{2,1},{3,2},{5,4},{6,5},{7,6},{9,8},{10,9},{11,10},{13,12},{... | collective-permute-start | bytes 49160 | tf_op jit(solution)/shard_map/ppermute | solution.py:433
  82.7 2.7 %collective-permute-done.7.refs_4_ = bf16[64,128]{1,0:T(8,128)(2,1)S(1)} collective-permute-done((bf16[64,128]{1,0:T(8,128)(2,1)S(1)}, bf16[64,128]{1,0:T(8,128)(2,1)S(1)}, u32[]{:S(2)}, u32[]{:S(2)}) %collective-permute-start.7) | collective-permute-done | bytes 16416 | tf_op jit(solution)/shard_map/ppermute | solution.py:433
  85.4 14.2 %backward.1 = (bf16[1152,128]{1,0:T(8,128)(2,1)S(1)}, bf16[128,128]{1,0:T(8,128)(2,1)S(1)}) custom-call(bf16[32,64,256]{2,1,0:T(8,128)(2,1)S(1)} %error_rows.1.mid_ref.refs_0_, bf16[1,64,256]{2,1,0:T(8,128)(2,1)S(1)} %collective-permute-done.4.top_ref.refs_1_, bf16[1,64,256]{2,1,0:T(8,128)(2,1)S(1)} %collective-permute-done.5.bottom_ref.refs_2_, ...), custom_call_target="tpu_custom_call" | custom-call | tf_op jit(solution)/shard_map/backward/pallas_call | solution.py:393
  100.9 10.1 %all-to-all-start.1 = ((bf16[128,10,128]{2,1,0:T(8,128)(2,1)}), bf16[128,10,128]{2,1,0:T(8,128)(2,1)S(1)}, u32[]{:S(2)}, u32[]{:S(2)}) async-start(bf16[128,10,128]{2,1,0:T(8,128)(2,1)} %pad_maximum_fusion), calls=%async_computation.1 | async-start | bytes 1048576 | tf_op jit(solution)/shard_map/all_to_all | solution.py:450
  111.0 14.1 %all-to-all-done.1 = bf16[128,10,128]{2,1,0:T(8,128)(2,1)S(1)} async-done(((bf16[128,10,128]{2,1,0:T(8,128)(2,1)}), bf16[128,10,128]{2,1,0:T(8,128)(2,1)S(1)}, u32[]{:S(2)}, u32[]{:S(2)}) %all-to-all-start.1) | async-done | bytes 327712 | tf_op jit(solution)/shard_map/all_to_all | solution.py:450
  126.4 3.6 %all-to-all-start.2 = ((bf16[128,10,128]{2,1,0:T(8,128)(2,1)}), bf16[128,10,128]{2,1,0:T(8,128)(2,1)S(1)}, u32[]{:S(2)}, u32[]{:S(2)}) async-start(bf16[128,10,128]{2,1,0:T(8,128)(2,1)} %broadcast_in_dim.5), calls=%async_computation.2 | async-start | bytes 1048576 | tf_op jit(solution)/shard_map/all_to_all | solution.py:456
  130.0 1.6 %copy.93 = bf16[64,32,256]{2,1,0:T(8,128)(2,1)} copy(bf16[64,32,256]{2,0,1:T(8,128)(2,1)S(1)} %bitcast.77) | data formatting | bytes 2097152
  131.6 12.7 %all-to-all-done.2 = bf16[128,10,128]{2,1,0:T(8,128)(2,1)S(1)} async-done(((bf16[128,10,128]{2,1,0:T(8,128)(2,1)}), bf16[128,10,128]{2,1,0:T(8,128)(2,1)S(1)}, u32[]{:S(2)}, u32[]{:S(2)}) %all-to-all-start.2) | async-done | bytes 327712 | tf_op jit(solution)/shard_map/all_to_all | solution.py:456
  (91 shorter events, 11.4 us)
Async XLA Ops:
  0.6 9.7 %copy-start = (s32[32,4]{0,1:T(4,128)S(1)}, s32[32,4]{0,1:T(4,128)}, u32[]{:S(2)}) copy-start(s32[32,4]{0,1:T(4,128)} %param.12) | copy-start | bytes 1540
  0.6 9.7 %copy-start.5 = (s32[32,4,8]{0,2,1:T(8,128)S(1)}, s32[32,4,8]{0,2,1:T(8,128)}, u32[]{:S(2)}) copy-start(s32[32,4,8]{0,2,1:T(8,128)} %param.11) | copy-start | bytes 12292
  3.4 12.3 %collective-permute-start = (bf16[2,80,256]{2,1,0:T(8,128)(2,1)S(1)}, bf16[2,80,256]{2,1,0:T(8,128)(2,1)S(1)}, u32[]{:S(2)}, u32[]{:S(2)}) collective-permute-start(bf16[2,80,256]{2,1,0:T(8,128)(2,1)S(1)} %get-tuple-element.63), channel_id=1, source_target_pairs={{0,4},{4,8},{8,12},{12,16},{16,20},{20,24},{24,28},{28,32},{32,36}... | collective-permute-start | bytes 245768 | tf_op jit(solution)/shard_map/ppermute | solution.py:425
  8.4 7.4 %collective-permute-start.1 = (bf16[2,80,256]{2,1,0:T(8,128)(2,1)S(1)}, bf16[2,80,256]{2,1,0:T(8,128)(2,1)S(1)}, u32[]{:S(2)}, u32[]{:S(2)}) collective-permute-start(bf16[2,80,256]{2,1,0:T(8,128)(2,1)S(1)} %get-tuple-element.62), channel_id=1, source_target_pairs={{4,0},{8,4},{12,8},{16,12},{20,16},{24,20},{28,24},{32,28},{36,32}... | collective-permute-start | bytes 245768 | tf_op jit(solution)/shard_map/ppermute | solution.py:426
  11.5 9.3 %copy-start.2 = (bf16[256,8192]{1,0:T(8,128)(2,1)S(1)}, bf16[256,8192]{1,0:T(8,128)(2,1)}, u32[]{:S(2)}) copy-start(bf16[256,8192]{1,0:T(8,128)(2,1)} %param.10) | copy-start | bytes 12582916
  16.4 9.4 %collective-permute-start.2 = (bf16[80,128]{1,0:T(8,128)(2,1)S(1)}, bf16[80,128]{1,0:T(8,128)(2,1)S(1)}, u32[]{:S(2)}, u32[]{:S(2)}) collective-permute-start(bf16[80,128]{1,0:T(8,128)(2,1)S(1)} %get-tuple-element.69), channel_id=1, source_target_pairs={{0,1},{1,2},{2,3},{4,5},{5,6},{6,7},{8,9},{9,10},{10,11},{12,13},{... | collective-permute-start | bytes 61448 | tf_op jit(solution)/shard_map/ppermute | solution.py:432
  19.5 6.3 %collective-permute-start.3 = (bf16[80,128]{1,0:T(8,128)(2,1)S(1)}, bf16[80,128]{1,0:T(8,128)(2,1)S(1)}, u32[]{:S(2)}, u32[]{:S(2)}) collective-permute-start(bf16[80,128]{1,0:T(8,128)(2,1)S(1)} %get-tuple-element.68), channel_id=1, source_target_pairs={{1,0},{2,1},{3,2},{5,4},{6,5},{7,6},{9,8},{10,9},{11,10},{13,12},{... | collective-permute-start | bytes 61448 | tf_op jit(solution)/shard_map/ppermute | solution.py:433
  27.2 31.1 %all-to-all-start = ((bf16[32,2,8192]{2,1,0:T(2,128)(2,1)}), bf16[32,2,8192]{2,1,0:T(2,128)(2,1)S(1)}, u32[]{:S(2)}, u32[]{:S(2)}) async-start(bf16[32,2,8192]{2,1,0:T(2,128)(2,1)} %reshape.278), calls=%async_computation | async-start | bytes 2097152 | tf_op jit(solution)/shard_map/all_to_all | solution.py:507
  35.8 7.8 %copy-start.6 = (f32[16,128]{1,0:T(8,128)S(1)}, f32[16,128]{1,0:T(8,128)}, u32[]{:S(2)}) copy-start(f32[16,128]{1,0:T(8,128)} %param.18) | copy-start | bytes 24580
  35.9 7.8 %copy-start.7 = (f32[16,128]{1,0:T(8,128)S(1)}, f32[16,128]{1,0:T(8,128)}, u32[]{:S(2)}) copy-start(f32[16,128]{1,0:T(8,128)} %param.19) | copy-start | bytes 24580
  35.9 7.9 %copy-start.3 = (bf16[64,128,3,3]{1,0,3,2:T(8,128)(2,1)S(1)}, bf16[64,128,3,3]{1,0,3,2:T(8,128)(2,1)}, u32[]{:S(2)}) copy-start(bf16[64,128,3,3]{1,0,3,2:T(8,128)(2,1)} %param.17) | copy-start | bytes 442372
  35.9 8.2 %copy-start.4 = (bf16[128,64,3,3]{0,1,3,2:T(8,128)(2,1)S(1)}, bf16[128,64,3,3]{0,1,3,2:T(8,128)(2,1)}, u32[]{:S(2)}) copy-start(bf16[128,64,3,3]{0,1,3,2:T(8,128)(2,1)} %param.16) | copy-start | bytes 442372
  67.4 5.5 %collective-permute-start.4 = (bf16[1,64,256]{2,1,0:T(8,128)(2,1)S(1)}, bf16[1,64,256]{2,1,0:T(8,128)(2,1)S(1)}, u32[]{:S(2)}, u32[]{:S(2)}) collective-permute-start(bf16[1,64,256]{2,1,0:T(8,128)(2,1)S(1)} %get-tuple-element.67), channel_id=1, source_target_pairs={{0,4},{4,8},{8,12},{12,16},{16,20},{20,24},{24,28},{28,32},{32,36}... | collective-permute-start | bytes 98312 | tf_op jit(solution)/shard_map/ppermute | solution.py:425
  70.9 5.2 %collective-permute-start.5 = (bf16[1,64,256]{2,1,0:T(8,128)(2,1)S(1)}, bf16[1,64,256]{2,1,0:T(8,128)(2,1)S(1)}, u32[]{:S(2)}, u32[]{:S(2)}) collective-permute-start(bf16[1,64,256]{2,1,0:T(8,128)(2,1)S(1)} %get-tuple-element.66), channel_id=1, source_target_pairs={{4,0},{8,4},{12,8},{16,12},{20,16},{24,20},{28,24},{32,28},{36,32}... | collective-permute-start | bytes 98312 | tf_op jit(solution)/shard_map/ppermute | solution.py:426
  76.7 6.0 %collective-permute-start.6 = (bf16[64,128]{1,0:T(8,128)(2,1)S(1)}, bf16[64,128]{1,0:T(8,128)(2,1)S(1)}, u32[]{:S(2)}, u32[]{:S(2)}) collective-permute-start(bf16[64,128]{1,0:T(8,128)(2,1)S(1)} %get-tuple-element.71), channel_id=1, source_target_pairs={{0,1},{1,2},{2,3},{4,5},{5,6},{6,7},{8,9},{9,10},{10,11},{12,13},{... | collective-permute-start | bytes 49160 | tf_op jit(solution)/shard_map/ppermute | solution.py:432
  81.0 4.5 %collective-permute-start.7 = (bf16[64,128]{1,0:T(8,128)(2,1)S(1)}, bf16[64,128]{1,0:T(8,128)(2,1)S(1)}, u32[]{:S(2)}, u32[]{:S(2)}) collective-permute-start(bf16[64,128]{1,0:T(8,128)(2,1)S(1)} %get-tuple-element.70), channel_id=1, source_target_pairs={{1,0},{2,1},{3,2},{5,4},{6,5},{7,6},{9,8},{10,9},{11,10},{13,12},{... | collective-permute-start | bytes 49160 | tf_op jit(solution)/shard_map/ppermute | solution.py:433
  100.9 24.2 %all-to-all-start.1 = ((bf16[128,10,128]{2,1,0:T(8,128)(2,1)}), bf16[128,10,128]{2,1,0:T(8,128)(2,1)S(1)}, u32[]{:S(2)}, u32[]{:S(2)}) async-start(bf16[128,10,128]{2,1,0:T(8,128)(2,1)} %pad_maximum_fusion), calls=%async_computation.1 | async-start | bytes 1048576 | tf_op jit(solution)/shard_map/all_to_all | solution.py:450
  126.4 17.9 %all-to-all-start.2 = ((bf16[128,10,128]{2,1,0:T(8,128)(2,1)}), bf16[128,10,128]{2,1,0:T(8,128)(2,1)S(1)}, u32[]{:S(2)}, u32[]{:S(2)}) async-start(bf16[128,10,128]{2,1,0:T(8,128)(2,1)} %broadcast_in_dim.5), calls=%async_computation.2 | async-start | bytes 1048576 | tf_op jit(solution)/shard_map/all_to_all | solution.py:456
  144.3 2.7 %copy-start.1 = (s32[32,4]{0,1:T(4,128)S(1)}, s32[32,4]{0,1:T(4,128)}, u32[]{:S(2)}) copy-start(s32[32,4]{0,1:T(4,128)} %param.12) | copy-start | bytes 1540

commit v3 on v2

--- a/solution.py
+++ b/solution.py
@@ -97,7 +97,7 @@
     return jnp.where(cls == (iota(cls.shape, 0) + 1).astype(F32), 1.0, 0.0).astype(BF16)
 
 
-STEP = 4
+STEP = 8
 
 
 def prepare_forward(
@@ -157,8 +157,8 @@
 
 
 def forward_body(
-    mid_ref, top_ref, bottom_ref, own_ref, left_ref, right_ref, w1_ref, gs_ref, w2_ref,
-    xs_out, first_ref, slope_ref, hidden_ref, onehot_ref, total_ref, xs_ref, hs_ref, split_ref, halo_ref,
+    mid_ref, top_ref, bottom_ref, own_ref, left_ref, right_ref, w1_ref, gs_ref, w2_ref, wb_ref, blocks_ref, weights_ref,
+    xs_ref, first_ref, slope_ref, hidden_ref, onehot_ref, error_ref, wb_out, gain_out, hs_ref, split_ref, halo_ref,
 ):
     rows = mid_ref.shape[0]
     step = pl.program_id(0)
@@ -168,9 +168,8 @@
         prepare_forward(
             mid_ref, top_ref, bottom_ref, own_ref, left_ref, right_ref, w1_ref, gs_ref, xs_ref, split_ref, halo_ref
         )
-
-    block = STEP * XS_ROW
-    xs_out[...] = xs_ref[pl.ds(pl.multiple_of(step * block, 16), block), :]
+        wb_out[...] = wb_ref[...]
+        gain_out[...] = split_ref[pl.ds(0, 128), :]
 
     def activate(hs, keep):
         done = []
@@ -188,16 +187,16 @@
             before, after = shifted(center, hidden_halo, h)
             slope = sigma * (1.0 + pre * (1.0 - sigma)) if keep else None
             done.append((h, first, slope, before, center, after, hot))
-        for k, (h, first, slope, before, center, after, hot) in enumerate(done):
+        for h, first, slope, before, center, after, hot in done:
             at = h * 384 if isinstance(h, int) else pl.multiple_of(h * 384, 16)
             hs_ref[pl.ds(at, 128), :] = before
             hs_ref[pl.ds(at + 128, 128), :] = center
             hs_ref[pl.ds(at + 256, 128), :] = after
             if keep:
-                first_ref[k] = first
-                slope_ref[k] = slope
-                hidden_ref[k] = center
-                onehot_ref[k] = hot
+                first_ref[h - 1] = first
+                slope_ref[h - 1] = slope
+                hidden_ref[h - 1] = center
+                onehot_ref[h - 1] = hot
 
     @pl.when(step == 0)
     def _():
@@ -213,44 +212,39 @@
         for k in range(STEP):
             r = (step - 1) * STEP + k
             stack = hs_ref[pl.ds(pl.multiple_of(r * 384, 16), 1152), :]
-            sums.append(dot(w2_ref[...], stack) + mid_ref[r][:64].astype(F32))
+            second = dot(w2_ref[...], stack)
+            target = dot(blocks_ref[...], weights_ref[k])
+            sums.append((mid_ref[r][:64].astype(F32) + second - target).astype(BF16))
         for k in range(STEP):
-            total_ref[k] = sums[k]
-
-
-def forward(mid, top, bottom, own, left, right, w1, gs, w2):
+            error_ref[(step - 1) * STEP + k] = sums[k]
+
+
+def forward(mid, top, bottom, own, left, right, w1, gs, w2, wb, blocks, weights):
     rows = mid.shape[0]
-    last = rows // STEP - 1
-
-    def block(shape):
-        return pl.BlockSpec((STEP,) + shape, lambda i: (jnp.minimum(i, last), 0, 0))
-
     return pl.pallas_call(
         forward_body,
         grid=(rows // STEP + 1,),
         out_shape=(
-            pltpu.HBM(((rows + 4) * XS_ROW, 256), BF16),
-            pltpu.HBM((rows, 128, 256), F32),
-            pltpu.HBM((rows, 128, 256), F32),
-            pltpu.HBM((rows, 128, 256), BF16),
-            pltpu.HBM((rows, 16, 256), BF16),
-            pltpu.HBM((rows, 64, 256), F32),
+            pltpu.VMEM(((rows + 4) * XS_ROW, 256), BF16),
+            pltpu.VMEM((rows, 128, 256), F32),
+            pltpu.VMEM((rows, 128, 256), F32),
+            pltpu.VMEM((rows, 128, 256), BF16),
+            pltpu.VMEM((rows, 16, 256), BF16),
+            pltpu.VMEM((rows, 64, 256), BF16),
+            pltpu.VMEM((128, 576), BF16),
+            pltpu.VMEM((128, 48), BF16),
         ),
-        in_specs=[whole()] * 9,
-        out_specs=(
-            pl.BlockSpec((STEP * XS_ROW, 256), lambda i: (i, 0)),
-            block((128, 256)), block((128, 256)), block((128, 256)), block((16, 256)),
-            pl.BlockSpec((STEP, 64, 256), lambda i: (jnp.maximum(i - 1, 0), 0, 0)),
-        ),
+        in_specs=[whole()] * 11
+        + [pl.BlockSpec((STEP,) + weights.shape[1:], lambda i: (jnp.maximum(i - 1, 0), 0, 0))],
+        out_specs=(whole(),) * 8,
         scratch_shapes=[
-            pltpu.VMEM(((rows + 4) * XS_ROW, 256), BF16),
             pltpu.VMEM(((rows + 2) * 384, 256), BF16),
             pltpu.VMEM((256, 48), BF16),
             pltpu.VMEM((3, 64, 128), BF16),
         ],
-        compiler_params=params(28),
+        compiler_params=params(26),
         name="forward",
-    )(mid, top, bottom, own, left, right, w1, gs, w2)
+    )(mid, top, bottom, own, left, right, w1, gs, w2, wb, blocks, *in_hbm(weights))
 
 
 def rows_first(weights, start, stop):
@@ -271,37 +265,9 @@
     )(*in_hbm(weights))
 
 
-def error_rows(blocks, weights, total):
-    rows, channels, cols = total.shape
-    step = 8
-
-    def body(blocks_ref, *refs):
-        parts, total_ref, error_ref = refs[:-2], refs[-2], refs[-1]
-        for k in range(step):
-            value = total_ref[k]
-            at = 0
-            for part in parts:
-                depth = part.shape[1]
-                value -= dot(blocks_ref[:, at : at + depth], part[k])
-                at += depth
-            error_ref[k] = value.astype(BF16)
-
-    return pl.pallas_call(
-        body,
-        grid=(rows // step,),
-        in_specs=[pl.BlockSpec(blocks.shape, lambda i: (0, 0))]
-        + [pl.BlockSpec((step,) + w.shape[1:], lambda i: (i, 0, 0)) for w in weights]
-        + [pl.BlockSpec((step, channels, cols), lambda i: (i, 0, 0))],
-        out_specs=pl.BlockSpec((step, channels, cols), lambda i: (i, 0, 0)),
-        out_shape=jax.ShapeDtypeStruct((rows, channels, cols), BF16),
-        compiler_params=params(20),
-        name="error_rows",
-    )(blocks, *in_hbm(*weights, total))
-
-
 def backward_body(
-    scale, err_ref, top_ref, bottom_ref, left_ref, right_ref, xs_ref, xs_next, first_ref, slope_ref,
-    hidden_ref, onehot_ref, wb_ref, gain_ref, grads_ref, row_ref, es_ref, g1_ref, g2_ref, cls_ref, split_ref,
+    scale, err_ref, top_ref, bottom_ref, left_ref, right_ref, xs_ref, first_ref, slope_ref,
+    hidden_ref, onehot_ref, wb_ref, gain_ref, grads_ref, row_ref, es_ref, g1_ref, g2_ref, cls_ref,
 ):
     rows = err_ref.shape[0]
     step = pl.program_id(0)
@@ -325,37 +291,33 @@
         g1_ref[...] = jnp.zeros_like(g1_ref)
         g2_ref[...] = jnp.zeros_like(g2_ref)
         cls_ref[...] = jnp.zeros_like(cls_ref)
-        split_ref[...] = table_split(gain_ref[...])
-
-    split = split_ref[...]
+
+    split = gain_ref[...]
     stacks, acts, inputs, classes = [], [], [], []
     for k in range(STEP):
         r = step * STEP + k
         stack = es_ref[pl.ds(pl.multiple_of(r * 192, 16), 576), :]
         back = dot(wb_ref[...], stack)
-        delta = back * slope_ref[k] * scale
-        hot = onehot_ref[k]
+        delta = back * slope_ref[r] * scale
+        hot = onehot_ref[r]
         gain = dot(split, jnp.concatenate([hot, hot, hot], axis=0))
         acts.append((delta * gain).astype(BF16))
-        scaled_first = delta * first_ref[k]
+        scaled_first = delta * first_ref[r]
         d_high = delta.astype(BF16)
         d_low = (delta - d_high.astype(F32)).astype(BF16)
         f_high = scaled_first.astype(BF16)
         f_low = (scaled_first - f_high.astype(F32)).astype(BF16)
         classes.append(jnp.concatenate([d_high, d_low, f_high, f_low], axis=0))
-        pieces = []
-        for x in range(k + 1, k + 4):
-            ref, at = (xs_ref, x) if x < STEP else (xs_next, x - STEP)
-            pieces.append(ref[pl.ds(at * XS_ROW, 192), :])
+        pieces = [xs_ref[pl.ds(pl.multiple_of((r + 1 + x) * XS_ROW, 16), 192), :] for x in range(3)]
         inputs.append(jnp.concatenate(pieces, axis=0))
         stacks.append(stack)
 
     def across(parts):
         return jnp.concatenate(parts, axis=1)
 
-    hots = across([onehot_ref[k] for k in range(STEP)])
+    hots = across([onehot_ref[step * STEP + k] for k in range(STEP)])
     acc1 = g1_ref[...] + nt(across(inputs), across(acts))
-    acc2 = g2_ref[...] + nt(across(stacks), across([hidden_ref[k] for k in range(STEP)]))
+    acc2 = g2_ref[...] + nt(across(stacks), across([hidden_ref[step * STEP + k] for k in range(STEP)]))
     acc3 = cls_ref[...] + nt(hots, across(classes))
     g1_ref[...] = acc1
     g2_ref[...] = acc2
@@ -384,21 +346,13 @@
     def const(shape):
         return pl.BlockSpec(shape, lambda i: (0,) * len(shape))
 
-    def moving(shape):
-        return pl.BlockSpec((STEP,) + shape[1:], lambda i: (i, 0, 0))
-
     def body(*refs):
         backward_body(scale, *refs)
 
     return pl.pallas_call(
         body,
         grid=(rows // STEP,),
-        in_specs=[
-            const(err.shape), const(top.shape), const(bottom.shape), const(left.shape), const(right.shape),
-            pl.BlockSpec((STEP * XS_ROW, 256), lambda i: (i, 0)),
-            pl.BlockSpec((STEP * XS_ROW, 256), lambda i: (i + 1, 0)), moving(first.shape), moving(slope.shape), moving(hidden.shape),
-            moving(onehot.shape), const(wb.shape), const(gains.shape),
-        ],
+        in_specs=[whole()] * 12,
         out_specs=(const((1152, 128)), const((128, 128))),
         out_shape=(jax.ShapeDtypeStruct((1152, 128), BF16), jax.ShapeDtypeStruct((128, 128), BF16)),
         scratch_shapes=[
@@ -406,11 +360,10 @@
             pltpu.VMEM((576, 128), F32),
             pltpu.VMEM((576, 128), F32),
             pltpu.VMEM((16, 512), F32),
-            pltpu.VMEM((128, 48), BF16),
         ],
-        compiler_params=params(32),
+        compiler_params=params(14),
         name="backward",
-    )(err, top, bottom, left, right, *in_hbm(xs, xs, first, slope, hidden, onehot), wb, gains)
+    )(err, top, bottom, left, right, xs, first, slope, hidden, onehot, wb, gains)
 
 
 def shifts(axis):
@@ -485,11 +438,9 @@
     )
     top, bottom = row_halo(mid, 2)
     weights = intersection_weights.reshape(-1, rows, cols)
-    deep = weights.shape[0]
-    cuts = (0, deep // 4, deep // 2, deep)
-    parts = [rows_first(weights, x, y) for x, y in zip(cuts, cuts[1:])]
-    top, bottom, parts[0] = lax.optimization_barrier((top, bottom, parts[0]))
+    weights = rows_first(weights, 0, weights.shape[0])
     own = pack_columns(mid, top, bottom, 2)
+    own, weights = lax.optimization_barrier((own, weights))
     left, right = column_halo(own)
 
     ids = lax.dynamic_index_in_dim(intersection_ids, column, 1, keepdims=False)
@@ -503,7 +454,6 @@
     mine = (live & (owner == band))[:, None, :] & (rank[:, None, :] == which)
     pick = (mine[..., None] & (local[:, None, :, None] == jnp.arange(held))).any(2)
     outgoing = dot(pick.reshape(2 * n_bands, held).astype(BF16), teacher).astype(BF16)
-    outgoing, left, right, parts[1] = lax.optimization_barrier((outgoing, left, right, parts[1]))
     incoming = lax.all_to_all(
         outgoing.reshape(n_bands, 2, -1), "wide", split_axis=0, concat_axis=0, tiled=True
     )
@@ -513,7 +463,6 @@
     wb = jnp.flip(conv_second, (2, 3)).transpose(1, 2, 3, 0).reshape(128, 576)
     gain3 = jnp.tile(class_gain.T, (1, 3))
     gs = jnp.concatenate([gain3, jnp.tile(class_shift.T, (1, 3))], axis=0)
-    xs, first, slope, hidden, onehot, total = forward(mid, top, bottom, own, left, right, w1, gs, w2)
 
     my_owner = lax.dynamic_index_in_dim(owner, band, 0, keepdims=False)
     my_live = lax.dynamic_index_in_dim(live, band, 0, keepdims=False)
@@ -523,13 +472,15 @@
     blocks = dot(take, incoming.reshape(2 * n_bands, -1)).astype(BF16)
     blocks = blocks.reshape(slots * depth, -1).T
 
-    err = error_rows(blocks, parts, total)
+    xs, first, slope, hidden, onehot, err, wb, gains = forward(
+        mid, top, bottom, own, left, right, w1, gs, w2, wb, blocks, weights
+    )
     error_field = err.transpose(1, 0, 2)
     e_top, e_bottom = row_halo(err, 1)
     e_left, e_right = column_halo(pack_columns(err, e_top, e_bottom, 1))
     scale = 1.0 / (rows * cols)
     grads, class_rows = backward(
-        scale, err, e_top, e_bottom, e_left, e_right, xs, first, slope, hidden, onehot, wb, gain3
+        scale, err, e_top, e_bottom, e_left, e_right, xs, first, slope, hidden, onehot, wb, gains
     )
     grads, classes = everywhere_sum(grads, class_rows)
     grad_first = grads[:576].reshape(3, 3, 64, 128).transpose(3, 2, 0, 1)

time: 148 us -> 144 us (0.973)
  Pallas kernels: 53.2 us -> 42.4 us
  matrix products: 1.14 us -> 4.55 us
  starting transfers between devices: 44.8 us -> 46.8 us
  other arithmetic: 3.13 us -> 5.1 us
    pallas_call x3 -> x2, Pallas kernels: 35.9 us -> 26.2 us  [the longest x1 14.6 us: forward(): pl.pallas_call(forward_body, grid=(rows // STEP + 1,), out_shape=(pltpu.V...]
    dot_general x2, matrix products: 1.14 us -> 4.55 us  [dot(): return jnp.dot(a, b, preferred_element_type=F32)]
    all_to_all x1, starting transfers between devices: 10.1 us -> 12.2 us  [everywhere_sum(): got = lax.all_to_all(table, axes, 0, 0, tiled=True)]
    pallas_call x3 -> x1, Pallas kernels: 16.1 us -> 15.1 us  [rows_first(): pl.pallas_call(body, grid=((stop - start) // chunk,), in_specs=[pl.BlockS...]
  transfers between devices with their start and end apart: 11 -> 11, of which waited for: 4 -> 5; matrix products, arithmetic and copies ran while one was open for 3% -> 4% of each run, Pallas kernels for 20% -> 11%
where the time goes in v3:
time: 144 us
  starting transfers between devices  46.8 us (32%)
  Pallas kernels  42.4 us (29%)
  waiting for transfers between devices  33.1 us (23%)
  local copies, waits for them, and re-layouts  10.3 us (7%)
  other arithmetic  5.1 us (4%)
  matrix products  4.55 us (3%)
    pallas_call x1, Pallas kernels, rows_first(): pl.pallas_call(body, grid=((stop - start) // chunk,), in_specs=[pl.BlockS...  15.1 us
    pallas_call x1, Pallas kernels, forward(): pl.pallas_call(forward_body, grid=(rows // STEP + 1,), out_shape=(pltpu.V...  14.6 us
    all_to_all x1, waiting for transfers between devices, everywhere_sum(): got = lax.all_to_all(table, axes, 0, 0, tiled=True)  14.1 us
    all_to_all x1, waiting for transfers between devices, everywhere_sum(): lax.all_to_all(jnp.broadcast_to(row, (n,) + row.shape), axes, 0, 0, tiled...  12.7 us
    all_to_all x1, starting transfers between devices, everywhere_sum(): got = lax.all_to_all(table, axes, 0, 0, tiled=True)  12.2 us
    pallas_call x1, Pallas kernels, backward(): pl.pallas_call(body, grid=(rows // STEP,), in_specs=[whole()] * 12, out_s...  11.6 us
    all_to_all x1, starting transfers between devices, shards(): lax.all_to_all(outgoing.reshape(n_bands, 2, -1), 'wide', split_axis=0, co...  9.6 us
    ppermute x2, starting transfers between devices, row_halo(): top = lax.ppermute(mid[mid.shape[0] - width:], 'wide', up)  8.61 us
  transfers between devices with their start and end apart: 11, of which 5 were waited for; matrix products, arithmetic and copies ran while one was open for 4% of the time, Pallas kernels for 11%

profile of v3, /device:TPU:1, one launch (start us, length us, event | category | flops | bytes accessed | tf_op | source)
XLA Modules:
  0.0 143.5 jit_solution(1396037264558788061)
XLA Ops:
  4.5 3.0 %convolution_convert_fusion = bf16[64,8192]{1,0:T(8,128)(2,1)S(1)} fusion(pred[64,256]{1,0:T(32,128)(4,1)S(1)} %reshape.280, bf16[256,8192]{1,0:T(8,128)(2,1)} %param.10), kind=kOutput, calls=%fused_computation | convolution fusion | flops 268959744 | bytes 5259264 | tf_op jit(solution)/shard_map/dot_general | solution.py:22
  7.6 1.5 %reshape.281 = bf16[32,2,8192]{2,1,0:T(2,128)(2,1)} reshape(bf16[64,8192]{1,0:T(8,128)(2,1)S(1)} %convolution_convert_fusion) | data formatting | bytes 2097152 | tf_op jit(solution)/shard_map/reshape | solution.py:458
  9.1 9.6 %all-to-all-start = ((bf16[32,2,8192]{2,1,0:T(2,128)(2,1)}), bf16[32,2,8192]{2,1,0:T(2,128)(2,1)S(1)}, u32[]{:S(2)}, u32[]{:S(2)}) async-start(bf16[32,2,8192]{2,1,0:T(2,128)(2,1)} %reshape.281), calls=%async_computation | async-start | bytes 2097152 | tf_op jit(solution)/shard_map/all_to_all | solution.py:457
  19.5 3.5 %collective-permute-start = (bf16[2,80,256]{2,1,0:T(8,128)(2,1)S(1)}, bf16[2,80,256]{2,1,0:T(8,128)(2,1)S(1)}, u32[]{:S(2)}, u32[]{:S(2)}) collective-permute-start(bf16[2,80,256]{2,1,0:T(8,128)(2,1)S(1)} %get-tuple-element.57), channel_id=1, source_target_pairs={{0,4},{4,8},{8,12},{12,16},{16,20},{20,24},{24,28},{28,32},{32,36}... | collective-permute-start | bytes 245768 | tf_op jit(solution)/shard_map/ppermute | solution.py:378
  23.1 1.9 %collective-permute-start.1 = (bf16[2,80,256]{2,1,0:T(8,128)(2,1)S(1)}, bf16[2,80,256]{2,1,0:T(8,128)(2,1)S(1)}, u32[]{:S(2)}, u32[]{:S(2)}) collective-permute-start(bf16[2,80,256]{2,1,0:T(8,128)(2,1)S(1)} %get-tuple-element.56), channel_id=1, source_target_pairs={{4,0},{8,4},{12,8},{16,12},{20,16},{24,20},{28,24},{32,28},{36,32}... | collective-permute-start | bytes 245768 | tf_op jit(solution)/shard_map/ppermute | solution.py:379
  25.0 15.1 %rows_first.1.weights_ref = bf16[32,1024,256]{2,1,0:T(8,128)(2,1)} custom-call(bf16[1024,32,256]{2,1,0:T(8,128)(2,1)} %bitcast.80), custom_call_target="tpu_custom_call" | custom-call | tf_op jit(solution)/shard_map/rows_first/pallas_call | solution.py:257
  41.8 3.1 %collective-permute-start.2 = (bf16[80,128]{1,0:T(8,128)(2,1)S(1)}, bf16[80,128]{1,0:T(8,128)(2,1)S(1)}, u32[]{:S(2)}, u32[]{:S(2)}) collective-permute-start(bf16[80,128]{1,0:T(8,128)(2,1)S(1)} %get-tuple-element.63), channel_id=1, source_target_pairs={{0,1},{1,2},{2,3},{4,5},{5,6},{6,7},{8,9},{9,10},{10,11},{12,13},{... | collective-permute-start | bytes 61448 | tf_op jit(solution)/shard_map/ppermute | solution.py:385
  44.9 1.3 collective-permute-start.3
  46.2 1.2 reshape.282
  47.4 1.5 %convolution_convert_fusion.1 = bf16[8,8192]{1,0:T(8,128)(2,1)S(1)} fusion(bf16[64,8192]{1,0:T(8,128)(2,1)} %reshape.282, s32[8]{0:T(128)S(1)} %add_reduce_fusion, pred[8]{0:T(512)(128)(4,1)S(1)} %dynamic-slice_bitcast_fusion), kind=kOutput, calls=%fused_computation.1 | convolution fusion | flops 8455168 | bytes 1179688 | tf_op jit(solution)/shard_map/dot_general | solution.py:22
  49.4 14.6 %forward.1 = (bf16[7488,256]{1,0:T(8,128)(2,1)S(1)}, f32[32,128,256]{2,1,0:T(8,128)S(1)}, f32[32,128,256]{2,1,0:T(8,128)S(1)}, bf16[32,128,256]{2,1,0:T(8,128)(2...) custom-call(bf16[32,80,256]{2,1,0:T(8,128)(2,1)S(1)} %fusion.1.mid_r, ...), custom_call_target="tpu_custom_call" | custom-call | tf_op jit(solution)/shard_map/forward/pallas_call | solution.py:224
  64.0 5.1 %collective-permute-start.4 = (bf16[1,64,256]{2,1,0:T(8,128)(2,1)S(1)}, bf16[1,64,256]{2,1,0:T(8,128)(2,1)S(1)}, u32[]{:S(2)}, u32[]{:S(2)}) collective-permute-start(bf16[1,64,256]{2,1,0:T(8,128)(2,1)S(1)} %get-tuple-element.61), channel_id=1, source_target_pairs={{0,4},{4,8},{8,12},{12,16},{16,20},{20,24},{24,28},{28,32},{32,36}... | collective-permute-start | bytes 98312 | tf_op jit(solution)/shard_map/ppermute | solution.py:378
  69.1 1.9 %collective-permute-start.5 = (bf16[1,64,256]{2,1,0:T(8,128)(2,1)S(1)}, bf16[1,64,256]{2,1,0:T(8,128)(2,1)S(1)}, u32[]{:S(2)}, u32[]{:S(2)}) collective-permute-start(bf16[1,64,256]{2,1,0:T(8,128)(2,1)S(1)} %get-tuple-element.60), channel_id=1, source_target_pairs={{4,0},{8,4},{12,8},{16,12},{20,16},{24,20},{28,24},{32,28},{36,32}... | collective-permute-start | bytes 98312 | tf_op jit(solution)/shard_map/ppermute | solution.py:379
  71.0 3.3 %collective-permute-done.5.bottom_ref.refs_2_ = bf16[1,64,256]{2,1,0:T(8,128)(2,1)S(1)} collective-permute-done((bf16[1,64,256]{2,1,0:T(8,128)(2,1)S(1)}, bf16[1,64,256]{2,1,0:T(8,128)(2,1)S(1)}, u32[]{:S(2)}, u32[]{:S(2)}) %collective-permute-start.5) | collective-permute-done | bytes 32800 | tf_op jit(solution)/shard_map/ppermute | solution.py:379
  74.9 3.1 %collective-permute-start.6 = (bf16[64,128]{1,0:T(8,128)(2,1)S(1)}, bf16[64,128]{1,0:T(8,128)(2,1)S(1)}, u32[]{:S(2)}, u32[]{:S(2)}) collective-permute-start(bf16[64,128]{1,0:T(8,128)(2,1)S(1)} %get-tuple-element.65), channel_id=1, source_target_pairs={{0,1},{1,2},{2,3},{4,5},{5,6},{6,7},{8,9},{9,10},{10,11},{12,13},{... | collective-permute-start | bytes 49160 | tf_op jit(solution)/shard_map/ppermute | solution.py:385
  78.0 1.5 %collective-permute-start.7 = (bf16[64,128]{1,0:T(8,128)(2,1)S(1)}, bf16[64,128]{1,0:T(8,128)(2,1)S(1)}, u32[]{:S(2)}, u32[]{:S(2)}) collective-permute-start(bf16[64,128]{1,0:T(8,128)(2,1)S(1)} %get-tuple-element.64), channel_id=1, source_target_pairs={{1,0},{2,1},{3,2},{5,4},{6,5},{7,6},{9,8},{10,9},{11,10},{13,12},{... | collective-permute-start | bytes 49160 | tf_op jit(solution)/shard_map/ppermute | solution.py:386
  79.5 3.0 %collective-permute-done.7.refs_4_ = bf16[64,128]{1,0:T(8,128)(2,1)S(1)} collective-permute-done((bf16[64,128]{1,0:T(8,128)(2,1)S(1)}, bf16[64,128]{1,0:T(8,128)(2,1)S(1)}, u32[]{:S(2)}, u32[]{:S(2)}) %collective-permute-start.7) | collective-permute-done | bytes 16416 | tf_op jit(solution)/shard_map/ppermute | solution.py:386
  82.5 11.6 %backward.1 = (bf16[1152,128]{1,0:T(8,128)(2,1)S(1)}, bf16[128,128]{1,0:T(8,128)(2,1)S(1)}) custom-call(bf16[32,64,256]{2,1,0:T(8,128)(2,1)S(1)} %get-tuple-element.19.mid_ref.refs_0_, bf16[1,64,256]{2,1,0:T(8,128)(2,1)S(1)} %collective-permute-done.4.top_ref.refs_1_, bf16[1,64,256]{2,1,0:T(8,128)(2,1)S(1)} %collective-permute-done.5.bottom_ref.refs_2_, ...), custom_call_target="tpu_custom_call" | custom-call | tf_op jit(solution)/shard_map/backward/pallas_call | solution.py:352
  94.2 1.0 pad_maximum_fusion
  95.3 12.2 %all-to-all-start.1 = ((bf16[128,10,128]{2,1,0:T(8,128)(2,1)}), bf16[128,10,128]{2,1,0:T(8,128)(2,1)S(1)}, u32[]{:S(2)}, u32[]{:S(2)}) async-start(bf16[128,10,128]{2,1,0:T(8,128)(2,1)} %pad_maximum_fusion), calls=%async_computation.1 | async-start | bytes 1048576 | tf_op jit(solution)/shard_map/all_to_all | solution.py:403
  107.5 14.1 %all-to-all-done.1 = bf16[128,10,128]{2,1,0:T(8,128)(2,1)S(1)} async-done(((bf16[128,10,128]{2,1,0:T(8,128)(2,1)}), bf16[128,10,128]{2,1,0:T(8,128)(2,1)S(1)}, u32[]{:S(2)}, u32[]{:S(2)}) %all-to-all-start.1) | async-done | bytes 327712 | tf_op jit(solution)/shard_map/all_to_all | solution.py:403
  122.9 3.6 %all-to-all-start.2 = ((bf16[128,10,128]{2,1,0:T(8,128)(2,1)}), bf16[128,10,128]{2,1,0:T(8,128)(2,1)S(1)}, u32[]{:S(2)}, u32[]{:S(2)}) async-start(bf16[128,10,128]{2,1,0:T(8,128)(2,1)} %broadcast_in_dim.5), calls=%async_computation.2 | async-start | bytes 1048576 | tf_op jit(solution)/shard_map/all_to_all | solution.py:409
  126.5 1.6 %copy.89 = bf16[64,32,256]{2,1,0:T(8,128)(2,1)} copy(bf16[64,32,256]{2,0,1:T(8,128)(2,1)S(1)} %bitcast.77) | data formatting | bytes 2097152
  128.1 12.7 %all-to-all-done.2 = bf16[128,10,128]{2,1,0:T(8,128)(2,1)S(1)} async-done(((bf16[128,10,128]{2,1,0:T(8,128)(2,1)}), bf16[128,10,128]{2,1,0:T(8,128)(2,1)S(1)}, u32[]{:S(2)}, u32[]{:S(2)}) %all-to-all-start.2) | async-done | bytes 327712 | tf_op jit(solution)/shard_map/all_to_all | solution.py:409
  (87 shorter events, 11.3 us)
Async XLA Ops:
  0.6 1.4 copy-start
  7.6 11.1 %copy-start.2 = (bf16[64,32,256]{2,1,0:T(8,128)(2,1)S(1)}, bf16[64,32,256]{2,1,0:T(8,128)(2,1)}, u32[]{:S(2)}) copy-start(bf16[64,32,256]{2,1,0:T(8,128)(2,1)} %param.14) | copy-start | bytes 3145732
  7.6 11.7 %copy-start.5 = (s32[32,256]{1,0:T(8,128)S(1)}, s32[32,256]{1,0:T(8,128)}, u32[]{:S(2)}) copy-start(s32[32,256]{1,0:T(8,128)} %param.15) | copy-start | bytes 98308
  9.1 37.1 %all-to-all-start = ((bf16[32,2,8192]{2,1,0:T(2,128)(2,1)}), bf16[32,2,8192]{2,1,0:T(2,128)(2,1)S(1)}, u32[]{:S(2)}, u32[]{:S(2)}) async-start(bf16[32,2,8192]{2,1,0:T(2,128)(2,1)} %reshape.281), calls=%async_computation | async-start | bytes 2097152 | tf_op jit(solution)/shard_map/all_to_all | solution.py:457
  19.5 21.6 %collective-permute-start = (bf16[2,80,256]{2,1,0:T(8,128)(2,1)S(1)}, bf16[2,80,256]{2,1,0:T(8,128)(2,1)S(1)}, u32[]{:S(2)}, u32[]{:S(2)}) collective-permute-start(bf16[2,80,256]{2,1,0:T(8,128)(2,1)S(1)} %get-tuple-element.57), channel_id=1, source_target_pairs={{0,4},{4,8},{8,12},{12,16},{16,20},{20,24},{24,28},{28,32},{32,36}... | collective-permute-start | bytes 245768 | tf_op jit(solution)/shard_map/ppermute | solution.py:378
  23.1 18.1 %collective-permute-start.1 = (bf16[2,80,256]{2,1,0:T(8,128)(2,1)S(1)}, bf16[2,80,256]{2,1,0:T(8,128)(2,1)S(1)}, u32[]{:S(2)}, u32[]{:S(2)}) collective-permute-start(bf16[2,80,256]{2,1,0:T(8,128)(2,1)S(1)} %get-tuple-element.56), channel_id=1, source_target_pairs={{4,0},{8,4},{12,8},{16,12},{20,16},{24,20},{28,24},{32,28},{36,32}... | collective-permute-start | bytes 245768 | tf_op jit(solution)/shard_map/ppermute | solution.py:379
  25.0 15.2 %copy-start.3 = (bf16[64,128,3,3]{1,0,3,2:T(8,128)(2,1)S(1)}, bf16[64,128,3,3]{1,0,3,2:T(8,128)(2,1)}, u32[]{:S(2)}) copy-start(bf16[64,128,3,3]{1,0,3,2:T(8,128)(2,1)} %param.17) | copy-start | bytes 442372
  25.0 15.6 %copy-start.6 = (f32[16,128]{1,0:T(8,128)S(1)}, f32[16,128]{1,0:T(8,128)}, u32[]{:S(2)}) copy-start(f32[16,128]{1,0:T(8,128)} %param.19) | copy-start | bytes 24580
  25.0 15.6 %copy-start.7 = (f32[16,128]{1,0:T(8,128)S(1)}, f32[16,128]{1,0:T(8,128)}, u32[]{:S(2)}) copy-start(f32[16,128]{1,0:T(8,128)} %param.18) | copy-start | bytes 24580
  25.0 15.7 %copy-start.4 = (bf16[128,64,3,3]{0,1,3,2:T(8,128)(2,1)S(1)}, bf16[128,64,3,3]{0,1,3,2:T(8,128)(2,1)}, u32[]{:S(2)}) copy-start(bf16[128,64,3,3]{0,1,3,2:T(8,128)(2,1)} %param.16) | copy-start | bytes 442372
  41.8 7.6 %collective-permute-start.2 = (bf16[80,128]{1,0:T(8,128)(2,1)S(1)}, bf16[80,128]{1,0:T(8,128)(2,1)S(1)}, u32[]{:S(2)}, u32[]{:S(2)}) collective-permute-start(bf16[80,128]{1,0:T(8,128)(2,1)S(1)} %get-tuple-element.63), channel_id=1, source_target_pairs={{0,1},{1,2},{2,3},{4,5},{5,6},{6,7},{8,9},{9,10},{10,11},{12,13},{... | collective-permute-start | bytes 61448 | tf_op jit(solution)/shard_map/ppermute | solution.py:385
  44.9 4.5 %collective-permute-start.3 = (bf16[80,128]{1,0:T(8,128)(2,1)S(1)}, bf16[80,128]{1,0:T(8,128)(2,1)S(1)}, u32[]{:S(2)}, u32[]{:S(2)}) collective-permute-start(bf16[80,128]{1,0:T(8,128)(2,1)S(1)} %get-tuple-element.62), channel_id=1, source_target_pairs={{1,0},{2,1},{3,2},{5,4},{6,5},{7,6},{9,8},{10,9},{11,10},{13,12},{... | collective-permute-start | bytes 61448 | tf_op jit(solution)/shard_map/ppermute | solution.py:386
  64.0 7.0 %collective-permute-start.4 = (bf16[1,64,256]{2,1,0:T(8,128)(2,1)S(1)}, bf16[1,64,256]{2,1,0:T(8,128)(2,1)S(1)}, u32[]{:S(2)}, u32[]{:S(2)}) collective-permute-start(bf16[1,64,256]{2,1,0:T(8,128)(2,1)S(1)} %get-tuple-element.61), channel_id=1, source_target_pairs={{0,4},{4,8},{8,12},{12,16},{16,20},{20,24},{24,28},{28,32},{32,36}... | collective-permute-start | bytes 98312 | tf_op jit(solution)/shard_map/ppermute | solution.py:378
  69.1 5.2 %collective-permute-start.5 = (bf16[1,64,256]{2,1,0:T(8,128)(2,1)S(1)}, bf16[1,64,256]{2,1,0:T(8,128)(2,1)S(1)}, u32[]{:S(2)}, u32[]{:S(2)}) collective-permute-start(bf16[1,64,256]{2,1,0:T(8,128)(2,1)S(1)} %get-tuple-element.60), channel_id=1, source_target_pairs={{4,0},{8,4},{12,8},{16,12},{20,16},{24,20},{28,24},{32,28},{36,32}... | collective-permute-start | bytes 98312 | tf_op jit(solution)/shard_map/ppermute | solution.py:379
  74.9 4.6 %collective-permute-start.6 = (bf16[64,128]{1,0:T(8,128)(2,1)S(1)}, bf16[64,128]{1,0:T(8,128)(2,1)S(1)}, u32[]{:S(2)}, u32[]{:S(2)}) collective-permute-start(bf16[64,128]{1,0:T(8,128)(2,1)S(1)} %get-tuple-element.65), channel_id=1, source_target_pairs={{0,1},{1,2},{2,3},{4,5},{5,6},{6,7},{8,9},{9,10},{10,11},{12,13},{... | collective-permute-start | bytes 49160 | tf_op jit(solution)/shard_map/ppermute | solution.py:385
  78.0 4.5 %collective-permute-start.7 = (bf16[64,128]{1,0:T(8,128)(2,1)S(1)}, bf16[64,128]{1,0:T(8,128)(2,1)S(1)}, u32[]{:S(2)}, u32[]{:S(2)}) collective-permute-start(bf16[64,128]{1,0:T(8,128)(2,1)S(1)} %get-tuple-element.64), channel_id=1, source_target_pairs={{1,0},{2,1},{3,2},{5,4},{6,5},{7,6},{9,8},{10,9},{11,10},{13,12},{... | collective-permute-start | bytes 49160 | tf_op jit(solution)/shard_map/ppermute | solution.py:386
  95.3 26.3 %all-to-all-start.1 = ((bf16[128,10,128]{2,1,0:T(8,128)(2,1)}), bf16[128,10,128]{2,1,0:T(8,128)(2,1)S(1)}, u32[]{:S(2)}, u32[]{:S(2)}) async-start(bf16[128,10,128]{2,1,0:T(8,128)(2,1)} %pad_maximum_fusion), calls=%async_computation.1 | async-start | bytes 1048576 | tf_op jit(solution)/shard_map/all_to_all | solution.py:403
  122.9 17.9 %all-to-all-start.2 = ((bf16[128,10,128]{2,1,0:T(8,128)(2,1)}), bf16[128,10,128]{2,1,0:T(8,128)(2,1)S(1)}, u32[]{:S(2)}, u32[]{:S(2)}) async-start(bf16[128,10,128]{2,1,0:T(8,128)(2,1)} %broadcast_in_dim.5), calls=%async_computation.2 | async-start | bytes 1048576 | tf_op jit(solution)/shard_map/all_to_all | solution.py:409
  140.8 2.7 %copy-start.1 = (s32[32,4]{0,1:T(4,128)S(1)}, s32[32,4]{0,1:T(4,128)}, u32[]{:S(2)}) copy-start(s32[32,4]{0,1:T(4,128)} %param.12) | copy-start | bytes 1540

commit v4 on v3

--- a/solution.py
+++ b/solution.py
@@ -445,15 +445,17 @@
 
     ids = lax.dynamic_index_in_dim(intersection_ids, column, 1, keepdims=False)
     counts = lax.dynamic_index_in_dim(slot_counts, column, 1, keepdims=False)
-    owner, local = ids // held, ids % held
     slot = lax.broadcasted_iota(jnp.int32, (n_bands, slots), 1)
-    live = slot < counts[:, None]
-    same = (owner[:, :, None] == owner[:, None, :]) & live[:, None, :]
-    rank = (same & (slot[:1, None, :] < slot[:1, :, None])).sum(-1)
-    which = lax.broadcasted_iota(jnp.int32, (n_bands, 2, slots), 1)
-    mine = (live & (owner == band))[:, None, :] & (rank[:, None, :] == which)
-    pick = (mine[..., None] & (local[:, None, :, None] == jnp.arange(held))).any(2)
-    outgoing = dot(pick.reshape(2 * n_bands, held).astype(BF16), teacher).astype(BF16)
+    mine = (slot < counts[:, None]) & (lax.div(ids, held) == band)
+    code = slot * held + lax.rem(ids, held)
+    last = slots * held
+    early = jnp.where(mine, code, last).min(1)
+    late = jnp.where(mine, code, -1).max(1)
+    picked = jnp.stack(
+        [jnp.where(early < last, lax.rem(early, held), -1), jnp.where(late > early, lax.rem(late, held), -1)], axis=1
+    )
+    pick = (picked[:, :, None] == jnp.arange(held)).astype(BF16)
+    outgoing = dot(pick.reshape(2 * n_bands, held), teacher).astype(BF16)
     incoming = lax.all_to_all(
         outgoing.reshape(n_bands, 2, -1), "wide", split_axis=0, concat_axis=0, tiled=True
     )
@@ -464,9 +466,12 @@
     gain3 = jnp.tile(class_gain.T, (1, 3))
     gs = jnp.concatenate([gain3, jnp.tile(class_shift.T, (1, 3))], axis=0)
 
-    my_owner = lax.dynamic_index_in_dim(owner, band, 0, keepdims=False)
-    my_live = lax.dynamic_index_in_dim(live, band, 0, keepdims=False)
-    my_rank = lax.dynamic_index_in_dim(rank, band, 0, keepdims=False)
+    here = jnp.arange(n_bands) == band
+    my_owner = lax.div(jnp.where(here[:, None], ids, 0).sum(0), held)
+    my_slot = jnp.arange(slots)
+    my_live = my_slot < jnp.where(here, counts, 0).sum()
+    same = (my_owner[:, None] == my_owner[None, :]) & my_live[None, :]
+    my_rank = (same & (my_slot[None, :] < my_slot[:, None])).sum(1)
     pair = lax.broadcasted_iota(jnp.int32, (slots, 2 * n_bands), 1)
     take = ((pair == (my_owner * 2 + my_rank)[:, None]) & my_live[:, None]).astype(BF16)
     blocks = dot(take, incoming.reshape(2 * n_bands, -1)).astype(BF16)

time: 144 us -> 143 us (level)
  transfers between devices with their start and end apart: 11 -> 11, of which waited for: 5 -> 5; matrix products, arithmetic and copies ran while one was open for 4% -> 5% of each run, Pallas kernels for 11% -> 11%
where the time goes in v4:
time: 143 us; the launch traced here: 142 us
  starting transfers between devices  46.9 us (33%)
  Pallas kernels  42 us (29%)
  waiting for transfers between devices  33.1 us (23%)
  local copies, waits for them, and re-layouts  10.1 us (7%)
  matrix products  4.6 us (3%)
  other arithmetic  4.56 us (3%)
    pallas_call x1, Pallas kernels, rows_first(): pl.pallas_call(body, grid=((stop - start) // chunk,), in_specs=[pl.BlockS...  15.1 us
    pallas_call x1, Pallas kernels, forward(): pl.pallas_call(forward_body, grid=(rows // STEP + 1,), out_shape=(pltpu.V...  14.4 us
    all_to_all x1, waiting for transfers between devices, everywhere_sum(): got = lax.all_to_all(table, axes, 0, 0, tiled=True)  14.1 us
    all_to_all x1, waiting for transfers between devices, everywhere_sum(): lax.all_to_all(jnp.broadcast_to(row, (n,) + row.shape), axes, 0, 0, tiled...  12.7 us
    all_to_all x1, starting transfers between devices, everywhere_sum(): got = lax.all_to_all(table, axes, 0, 0, tiled=True)  12.1 us
    pallas_call x1, Pallas kernels, backward(): pl.pallas_call(body, grid=(rows // STEP,), in_specs=[whole()] * 12, out_s...  11.4 us
    all_to_all x1, starting transfers between devices, shards(): lax.all_to_all(outgoing.reshape(n_bands, 2, -1), 'wide', split_axis=0, co...  9.6 us
    ppermute x2, starting transfers between devices, row_halo(): top = lax.ppermute(mid[mid.shape[0] - width:], 'wide', up)  8.61 us
  transfers between devices with their start and end apart: 11, of which 5 were waited for; matrix products, arithmetic and copies ran while one was open for 5% of the time, Pallas kernels for 11%

profile of v4, /device:TPU:1, one launch (start us, length us, event | category | flops | bytes accessed | tf_op | source)
XLA Modules:
  0.0 142.3 jit_solution(753818044816356721)
XLA Ops:
  0.7 1.3 select_reduce_fusion.2
  3.1 3.1 %convolution_convert_fusion = bf16[64,8192]{1,0:T(8,128)(2,1)S(1)} fusion(bf16[256,8192]{1,0:T(8,128)(2,1)} %param.10, s32[64]{0:T(128)S(1)} %eq.62), kind=kOutput, calls=%fused_computation | convolution fusion | flops 268976128 | bytes 5243136 | tf_op jit(solution)/shard_map/dot_general | solution.py:22
  6.2 1.5 %reshape.220 = bf16[32,2,8192]{2,1,0:T(2,128)(2,1)} reshape(bf16[64,8192]{1,0:T(8,128)(2,1)S(1)} %convolution_convert_fusion) | data formatting | bytes 2097152 | tf_op jit(solution)/shard_map/reshape | solution.py:460
  7.7 9.6 %all-to-all-start = ((bf16[32,2,8192]{2,1,0:T(2,128)(2,1)}), bf16[32,2,8192]{2,1,0:T(2,128)(2,1)S(1)}, u32[]{:S(2)}, u32[]{:S(2)}) async-start(bf16[32,2,8192]{2,1,0:T(2,128)(2,1)} %reshape.220), calls=%async_computation | async-start | bytes 2097152 | tf_op jit(solution)/shard_map/all_to_all | solution.py:459
  18.1 3.5 %collective-permute-start = (bf16[2,80,256]{2,1,0:T(8,128)(2,1)S(1)}, bf16[2,80,256]{2,1,0:T(8,128)(2,1)S(1)}, u32[]{:S(2)}, u32[]{:S(2)}) collective-permute-start(bf16[2,80,256]{2,1,0:T(8,128)(2,1)S(1)} %get-tuple-element.55), channel_id=1, source_target_pairs={{0,4},{4,8},{8,12},{12,16},{16,20},{20,24},{24,28},{28,32},{32,36}... | collective-permute-start | bytes 245768 | tf_op jit(solution)/shard_map/ppermute | solution.py:378
  21.7 1.9 %collective-permute-start.1 = (bf16[2,80,256]{2,1,0:T(8,128)(2,1)S(1)}, bf16[2,80,256]{2,1,0:T(8,128)(2,1)S(1)}, u32[]{:S(2)}, u32[]{:S(2)}) collective-permute-start(bf16[2,80,256]{2,1,0:T(8,128)(2,1)S(1)} %get-tuple-element.54), channel_id=1, source_target_pairs={{4,0},{8,4},{12,8},{16,12},{20,16},{24,20},{28,24},{32,28},{36,32}... | collective-permute-start | bytes 245768 | tf_op jit(solution)/shard_map/ppermute | solution.py:379
  23.6 15.1 %rows_first.1.weights_ref = bf16[32,1024,256]{2,1,0:T(8,128)(2,1)} custom-call(bf16[1024,32,256]{2,1,0:T(8,128)(2,1)} %bitcast.72), custom_call_target="tpu_custom_call" | custom-call | tf_op jit(solution)/shard_map/rows_first/pallas_call | solution.py:257
  41.0 3.1 %collective-permute-start.2 = (bf16[80,128]{1,0:T(8,128)(2,1)S(1)}, bf16[80,128]{1,0:T(8,128)(2,1)S(1)}, u32[]{:S(2)}, u32[]{:S(2)}) collective-permute-start(bf16[80,128]{1,0:T(8,128)(2,1)S(1)} %get-tuple-element.61), channel_id=1, source_target_pairs={{0,1},{1,2},{2,3},{4,5},{5,6},{6,7},{8,9},{9,10},{10,11},{12,13},{... | collective-permute-start | bytes 61448 | tf_op jit(solution)/shard_map/ppermute | solution.py:385
  44.1 1.3 collective-permute-start.3
  45.5 1.2 reshape.221
  46.7 1.5 %convolution_convert_fusion.1 = bf16[8,8192]{1,0:T(8,128)(2,1)S(1)} fusion(bf16[64,8192]{1,0:T(8,128)(2,1)} %reshape.221, s32[8]{0:T(128)S(1)} %multiply_add_fusion, pred[8]{0:T(512)(128)(4,1)S(1)} %iota_compare_fusion.6), kind=kOutput, calls=%fused_computation.1 | convolution fusion | flops 8455168 | bytes 1179688 | tf_op jit(solution)/shard_map/dot_general | solution.py:22
  48.7 14.4 %forward.1 = (bf16[7488,256]{1,0:T(8,128)(2,1)S(1)}, f32[32,128,256]{2,1,0:T(8,128)S(1)}, f32[32,128,256]{2,1,0:T(8,128)S(1)}, bf16[32,128,256]{2,1,0:T(8,128)(2...) custom-call(bf16[32,80,256]{2,1,0:T(8,128)(2,1)S(1)} %fusion.1.mid_r, ...), custom_call_target="tpu_custom_call" | custom-call | tf_op jit(solution)/shard_map/forward/pallas_call | solution.py:224
  63.1 5.1 %collective-permute-start.4 = (bf16[1,64,256]{2,1,0:T(8,128)(2,1)S(1)}, bf16[1,64,256]{2,1,0:T(8,128)(2,1)S(1)}, u32[]{:S(2)}, u32[]{:S(2)}) collective-permute-start(bf16[1,64,256]{2,1,0:T(8,128)(2,1)S(1)} %get-tuple-element.59), channel_id=1, source_target_pairs={{0,4},{4,8},{8,12},{12,16},{16,20},{20,24},{24,28},{28,32},{32,36}... | collective-permute-start | bytes 98312 | tf_op jit(solution)/shard_map/ppermute | solution.py:378
  68.1 1.9 %collective-permute-start.5 = (bf16[1,64,256]{2,1,0:T(8,128)(2,1)S(1)}, bf16[1,64,256]{2,1,0:T(8,128)(2,1)S(1)}, u32[]{:S(2)}, u32[]{:S(2)}) collective-permute-start(bf16[1,64,256]{2,1,0:T(8,128)(2,1)S(1)} %get-tuple-element.58), channel_id=1, source_target_pairs={{4,0},{8,4},{12,8},{16,12},{20,16},{24,20},{28,24},{32,28},{36,32}... | collective-permute-start | bytes 98312 | tf_op jit(solution)/shard_map/ppermute | solution.py:379
  70.1 3.3 %collective-permute-done.5.bottom_ref.refs_2_ = bf16[1,64,256]{2,1,0:T(8,128)(2,1)S(1)} collective-permute-done((bf16[1,64,256]{2,1,0:T(8,128)(2,1)S(1)}, bf16[1,64,256]{2,1,0:T(8,128)(2,1)S(1)}, u32[]{:S(2)}, u32[]{:S(2)}) %collective-permute-start.5) | collective-permute-done | bytes 32800 | tf_op jit(solution)/shard_map/ppermute | solution.py:379
  73.9 3.1 %collective-permute-start.6 = (bf16[64,128]{1,0:T(8,128)(2,1)S(1)}, bf16[64,128]{1,0:T(8,128)(2,1)S(1)}, u32[]{:S(2)}, u32[]{:S(2)}) collective-permute-start(bf16[64,128]{1,0:T(8,128)(2,1)S(1)} %get-tuple-element.63), channel_id=1, source_target_pairs={{0,1},{1,2},{2,3},{4,5},{5,6},{6,7},{8,9},{9,10},{10,11},{12,13},{... | collective-permute-start | bytes 49160 | tf_op jit(solution)/shard_map/ppermute | solution.py:385
  77.0 1.5 %collective-permute-start.7 = (bf16[64,128]{1,0:T(8,128)(2,1)S(1)}, bf16[64,128]{1,0:T(8,128)(2,1)S(1)}, u32[]{:S(2)}, u32[]{:S(2)}) collective-permute-start(bf16[64,128]{1,0:T(8,128)(2,1)S(1)} %get-tuple-element.62), channel_id=1, source_target_pairs={{1,0},{2,1},{3,2},{5,4},{6,5},{7,6},{9,8},{10,9},{11,10},{13,12},{... | collective-permute-start | bytes 49160 | tf_op jit(solution)/shard_map/ppermute | solution.py:386
  78.5 3.0 %collective-permute-done.7.refs_4_ = bf16[64,128]{1,0:T(8,128)(2,1)S(1)} collective-permute-done((bf16[64,128]{1,0:T(8,128)(2,1)S(1)}, bf16[64,128]{1,0:T(8,128)(2,1)S(1)}, u32[]{:S(2)}, u32[]{:S(2)}) %collective-permute-start.7) | collective-permute-done | bytes 16416 | tf_op jit(solution)/shard_map/ppermute | solution.py:386
  81.5 11.4 %backward.1 = (bf16[1152,128]{1,0:T(8,128)(2,1)S(1)}, bf16[128,128]{1,0:T(8,128)(2,1)S(1)}) custom-call(bf16[32,64,256]{2,1,0:T(8,128)(2,1)S(1)} %get-tuple-element.19.mid_ref.refs_0_, bf16[1,64,256]{2,1,0:T(8,128)(2,1)S(1)} %collective-permute-done.4.top_ref.refs_1_, bf16[1,64,256]{2,1,0:T(8,128)(2,1)S(1)} %collective-permute-done.5.bottom_ref.refs_2_, ...), custom_call_target="tpu_custom_call" | custom-call | tf_op jit(solution)/shard_map/backward/pallas_call | solution.py:352
  94.1 12.1 %all-to-all-start.1 = ((bf16[128,10,128]{2,1,0:T(8,128)(2,1)}), bf16[128,10,128]{2,1,0:T(8,128)(2,1)S(1)}, u32[]{:S(2)}, u32[]{:S(2)}) async-start(bf16[128,10,128]{2,1,0:T(8,128)(2,1)} %pad_maximum_fusion), calls=%async_computation.1 | async-start | bytes 1048576 | tf_op jit(solution)/shard_map/all_to_all | solution.py:403
  106.3 14.1 %all-to-all-done.1 = bf16[128,10,128]{2,1,0:T(8,128)(2,1)S(1)} async-done(((bf16[128,10,128]{2,1,0:T(8,128)(2,1)}), bf16[128,10,128]{2,1,0:T(8,128)(2,1)S(1)}, u32[]{:S(2)}, u32[]{:S(2)}) %all-to-all-start.1) | async-done | bytes 327712 | tf_op jit(solution)/shard_map/all_to_all | solution.py:403
  121.7 3.6 %all-to-all-start.2 = ((bf16[128,10,128]{2,1,0:T(8,128)(2,1)}), bf16[128,10,128]{2,1,0:T(8,128)(2,1)S(1)}, u32[]{:S(2)}, u32[]{:S(2)}) async-start(bf16[128,10,128]{2,1,0:T(8,128)(2,1)} %broadcast_in_dim.51), calls=%async_computation.2 | async-start | bytes 1048576 | tf_op jit(solution)/shard_map/all_to_all | solution.py:409
  125.4 1.6 %copy.60 = bf16[64,32,256]{2,1,0:T(8,128)(2,1)} copy(bf16[64,32,256]{2,0,1:T(8,128)(2,1)S(1)} %bitcast.69) | data formatting | bytes 2097152
  126.9 12.7 %all-to-all-done.2 = bf16[128,10,128]{2,1,0:T(8,128)(2,1)S(1)} async-done(((bf16[128,10,128]{2,1,0:T(8,128)(2,1)}), bf16[128,10,128]{2,1,0:T(8,128)(2,1)S(1)}, u32[]{:S(2)}, u32[]{:S(2)}) %all-to-all-start.2) | async-done | bytes 327712 | tf_op jit(solution)/shard_map/all_to_all | solution.py:409
  (76 shorter events, 10.2 us)
Async XLA Ops:
  6.2 11.1 %copy-start = (bf16[64,32,256]{2,1,0:T(8,128)(2,1)S(1)}, bf16[64,32,256]{2,1,0:T(8,128)(2,1)}, u32[]{:S(2)}) copy-start(bf16[64,32,256]{2,1,0:T(8,128)(2,1)} %param.14) | copy-start | bytes 3145732
  6.2 11.7 %copy-start.3 = (s32[32,256]{1,0:T(8,128)S(1)}, s32[32,256]{1,0:T(8,128)}, u32[]{:S(2)}) copy-start(s32[32,256]{1,0:T(8,128)} %param.15) | copy-start | bytes 98308
  7.7 37.7 %all-to-all-start = ((bf16[32,2,8192]{2,1,0:T(2,128)(2,1)}), bf16[32,2,8192]{2,1,0:T(2,128)(2,1)S(1)}, u32[]{:S(2)}, u32[]{:S(2)}) async-start(bf16[32,2,8192]{2,1,0:T(2,128)(2,1)} %reshape.220), calls=%async_computation | async-start | bytes 2097152 | tf_op jit(solution)/shard_map/all_to_all | solution.py:459
  18.1 22.3 %collective-permute-start = (bf16[2,80,256]{2,1,0:T(8,128)(2,1)S(1)}, bf16[2,80,256]{2,1,0:T(8,128)(2,1)S(1)}, u32[]{:S(2)}, u32[]{:S(2)}) collective-permute-start(bf16[2,80,256]{2,1,0:T(8,128)(2,1)S(1)} %get-tuple-element.55), channel_id=1, source_target_pairs={{0,4},{4,8},{8,12},{12,16},{16,20},{20,24},{24,28},{28,32},{32,36}... | collective-permute-start | bytes 245768 | tf_op jit(solution)/shard_map/ppermute | solution.py:378
  21.7 18.8 %collective-permute-start.1 = (bf16[2,80,256]{2,1,0:T(8,128)(2,1)S(1)}, bf16[2,80,256]{2,1,0:T(8,128)(2,1)S(1)}, u32[]{:S(2)}, u32[]{:S(2)}) collective-permute-start(bf16[2,80,256]{2,1,0:T(8,128)(2,1)S(1)} %get-tuple-element.54), channel_id=1, source_target_pairs={{4,0},{8,4},{12,8},{16,12},{20,16},{24,20},{28,24},{32,28},{36,32}... | collective-permute-start | bytes 245768 | tf_op jit(solution)/shard_map/ppermute | solution.py:379
  23.6 15.2 %copy-start.1 = (bf16[64,128,3,3]{1,0,3,2:T(8,128)(2,1)S(1)}, bf16[64,128,3,3]{1,0,3,2:T(8,128)(2,1)}, u32[]{:S(2)}) copy-start(bf16[64,128,3,3]{1,0,3,2:T(8,128)(2,1)} %param.17) | copy-start | bytes 442372
  23.6 16.5 %copy-start.4 = (f32[16,128]{1,0:T(8,128)S(1)}, f32[16,128]{1,0:T(8,128)}, u32[]{:S(2)}) copy-start(f32[16,128]{1,0:T(8,128)} %param.19) | copy-start | bytes 24580
  23.6 16.5 %copy-start.5 = (f32[16,128]{1,0:T(8,128)S(1)}, f32[16,128]{1,0:T(8,128)}, u32[]{:S(2)}) copy-start(f32[16,128]{1,0:T(8,128)} %param.18) | copy-start | bytes 24580
  23.6 16.6 %copy-start.2 = (bf16[128,64,3,3]{0,1,3,2:T(8,128)(2,1)S(1)}, bf16[128,64,3,3]{0,1,3,2:T(8,128)(2,1)}, u32[]{:S(2)}) copy-start(bf16[128,64,3,3]{0,1,3,2:T(8,128)(2,1)} %param.16) | copy-start | bytes 442372
  41.0 7.6 %collective-permute-start.2 = (bf16[80,128]{1,0:T(8,128)(2,1)S(1)}, bf16[80,128]{1,0:T(8,128)(2,1)S(1)}, u32[]{:S(2)}, u32[]{:S(2)}) collective-permute-start(bf16[80,128]{1,0:T(8,128)(2,1)S(1)} %get-tuple-element.61), channel_id=1, source_target_pairs={{0,1},{1,2},{2,3},{4,5},{5,6},{6,7},{8,9},{9,10},{10,11},{12,13},{... | collective-permute-start | bytes 61448 | tf_op jit(solution)/shard_map/ppermute | solution.py:385
  44.1 4.5 %collective-permute-start.3 = (bf16[80,128]{1,0:T(8,128)(2,1)S(1)}, bf16[80,128]{1,0:T(8,128)(2,1)S(1)}, u32[]{:S(2)}, u32[]{:S(2)}) collective-permute-start(bf16[80,128]{1,0:T(8,128)(2,1)S(1)} %get-tuple-element.60), channel_id=1, source_target_pairs={{1,0},{2,1},{3,2},{5,4},{6,5},{7,6},{9,8},{10,9},{11,10},{13,12},{... | collective-permute-start | bytes 61448 | tf_op jit(solution)/shard_map/ppermute | solution.py:386
  63.1 7.0 %collective-permute-start.4 = (bf16[1,64,256]{2,1,0:T(8,128)(2,1)S(1)}, bf16[1,64,256]{2,1,0:T(8,128)(2,1)S(1)}, u32[]{:S(2)}, u32[]{:S(2)}) collective-permute-start(bf16[1,64,256]{2,1,0:T(8,128)(2,1)S(1)} %get-tuple-element.59), channel_id=1, source_target_pairs={{0,4},{4,8},{8,12},{12,16},{16,20},{20,24},{24,28},{28,32},{32,36}... | collective-permute-start | bytes 98312 | tf_op jit(solution)/shard_map/ppermute | solution.py:378
  68.1 5.2 %collective-permute-start.5 = (bf16[1,64,256]{2,1,0:T(8,128)(2,1)S(1)}, bf16[1,64,256]{2,1,0:T(8,128)(2,1)S(1)}, u32[]{:S(2)}, u32[]{:S(2)}) collective-permute-start(bf16[1,64,256]{2,1,0:T(8,128)(2,1)S(1)} %get-tuple-element.58), channel_id=1, source_target_pairs={{4,0},{8,4},{12,8},{16,12},{20,16},{24,20},{28,24},{32,28},{36,32}... | collective-permute-start | bytes 98312 | tf_op jit(solution)/shard_map/ppermute | solution.py:379
  73.9 4.6 %collective-permute-start.6 = (bf16[64,128]{1,0:T(8,128)(2,1)S(1)}, bf16[64,128]{1,0:T(8,128)(2,1)S(1)}, u32[]{:S(2)}, u32[]{:S(2)}) collective-permute-start(bf16[64,128]{1,0:T(8,128)(2,1)S(1)} %get-tuple-element.63), channel_id=1, source_target_pairs={{0,1},{1,2},{2,3},{4,5},{5,6},{6,7},{8,9},{9,10},{10,11},{12,13},{... | collective-permute-start | bytes 49160 | tf_op jit(solution)/shard_map/ppermute | solution.py:385
  77.0 4.5 %collective-permute-start.7 = (bf16[64,128]{1,0:T(8,128)(2,1)S(1)}, bf16[64,128]{1,0:T(8,128)(2,1)S(1)}, u32[]{:S(2)}, u32[]{:S(2)}) collective-permute-start(bf16[64,128]{1,0:T(8,128)(2,1)S(1)} %get-tuple-element.62), channel_id=1, source_target_pairs={{1,0},{2,1},{3,2},{5,4},{6,5},{7,6},{9,8},{10,9},{11,10},{13,12},{... | collective-permute-start | bytes 49160 | tf_op jit(solution)/shard_map/ppermute | solution.py:386
  94.1 26.3 %all-to-all-start.1 = ((bf16[128,10,128]{2,1,0:T(8,128)(2,1)}), bf16[128,10,128]{2,1,0:T(8,128)(2,1)S(1)}, u32[]{:S(2)}, u32[]{:S(2)}) async-start(bf16[128,10,128]{2,1,0:T(8,128)(2,1)} %pad_maximum_fusion), calls=%async_computation.1 | async-start | bytes 1048576 | tf_op jit(solution)/shard_map/all_to_all | solution.py:403
  121.7 17.9 %all-to-all-start.2 = ((bf16[128,10,128]{2,1,0:T(8,128)(2,1)}), bf16[128,10,128]{2,1,0:T(8,128)(2,1)S(1)}, u32[]{:S(2)}, u32[]{:S(2)}) async-start(bf16[128,10,128]{2,1,0:T(8,128)(2,1)} %broadcast_in_dim.51), calls=%async_computation.2 | async-start | bytes 1048576 | tf_op jit(solution)/shard_map/all_to_all | solution.py:409
